TPU v7x, 256 devices: a whole 4x4x8 slice. The times are simulated.
256 devices in a mesh: dp: 4 (over y_hi, core), tm: 32 (over x, z), height: 2 (over y_lo).
Axes of the slice: x: 4, y: 4 (y_hi: 2, y_lo: 2; y = y_hi * 2 + y_lo), z: 8, core: 2. Of those that a mesh axis runs over, the one named last changes fastest.
Arguments:
- field: bfloat16 [4, 128, 18, 64, 640], P('dp', 'tm', 'height'), may hold values from -128 to 128, as said below
- cotangent: bfloat16 [4, 128, 18, 64, 640], P('dp', 'tm', 'height'), may hold values from -128 to 128, as said below
- gamma: float32 [640], replicated, may hold values from 0.1 to 1.9
- beta: float32 [640], replicated, may hold values from -2.5 to 2.5
- kernel: bfloat16 [3, 640, 640], replicated, may hold values from -0.125 to 0.125
Outputs:
- field_grad: bfloat16 [4, 128, 18, 64, 640], P('dp', 'tm', 'height')
- kernel_grad: float32 [1920, 640], P(('tm', 'height'), 'dp')
- channel_grads: float32 [3, 640], replicated
Inputs may be any that keep to these rules, and one draw needn't show every extreme that they name: `field`: activations of varying scale. `cotangent`: gradients of varying scale.
All inputs are finite; a program needn't handle non-finite values.
Results may differ from a plain program's by a relative error of at most 0.0045.
Values may be sent and summed in bfloat16 or wider, within the bound.
No kernel may reach another device: no remote copies, remote signals or barrier semaphores. Data moves between devices by JAX's collectives and lax.ppermute only.
A program may use at most 128 MiB of HBM per device.

v0:
```python
import functools
import math

import jax
import jax.numpy as jnp
from jax import lax
from jax.experimental import pallas as pl
from jax.experimental.pallas import tpu as pltpu
from jax.sharding import PartitionSpec as P

GROUPS = 32
CPG = 20
FRAME = 576
CHUNK = 768
CHAN_TOTAL = 128 * 18 * 64 * CPG
AXES = ("dp", "tm", "height")
BIT = {"yh": 7, "core": 6, "x1": 5, "x0": 4, "z2": 3, "z1": 2, "z0": 1, "yl": 0}
OWNER = ("x1", "x0", "z2", "z1", "z0", "yl")
ORDERS = (("z0", "x0", "yl", "x1", "z1"), ("yl", "z0", "x0", "x1", "z1"))
f32 = jnp.float32
bf16 = jnp.bfloat16
IN_VMEM = pl.BlockSpec(memory_space=pltpu.VMEM)
ANYWHERE = pl.BlockSpec(memory_space=pl.ANY)
IN_SMEM = pl.BlockSpec(memory_space=pltpu.SMEM)


def params(mib):
    return pltpu.CompilerParams(vmem_limit_bytes=mib * 2**20)


def vmem(shape, dtype):
    return pltpu.VMEM(shape, dtype)


def in_hbm(*arrays):
    return [pltpu.with_memory_space_constraint(array, pltpu.HBM) for array in arrays]


def cost(flops, moved, transcendentals=0):
    return pl.CostEstimate(flops=flops, bytes_accessed=moved, transcendentals=transcendentals)


def pairs(bits):
    mask = sum(1 << BIT[bit] for bit in bits)
    return [(i, i ^ mask) for i in range(256)]


def neighbours(axis):
    out = []
    for i in range(256):
        bit = {name: (i >> at) & 1 for name, at in BIT.items()}
        x, y = 2 * bit["x1"] + bit["x0"], 2 * bit["yh"] + bit["yl"]
        z = 4 * bit["z2"] + 2 * bit["z1"] + bit["z0"]
        place = {"x": x, "y": y, "z": z}
        size = 8 if axis == "z" else 4
        at = place[axis]
        step = 1 if (at % 2 == 0) == (bit["core"] == 0) else -1
        place[axis] = (at + step) % size
        x, y, z = place["x"], place["y"], place["z"]
        out.append((i, (((y >> 1) * 2 + bit["core"]) * 32 + x * 8 + z) * 2 + (y & 1)))
    return out


NEAR = {"z0": "z", "x0": "x", "yl": "y"}


def swap(value, *bits):
    chosen = pairs(bits)
    if bits == ("z1",):
        both = pairs(("z1", "z2"))
        chosen = [both[i] if (i >> BIT["core"]) & 1 else pair for i, pair in enumerate(chosen)]
    return lax.ppermute(value, AXES, chosen)


def half(total, axis, index):
    return lax.dynamic_index_in_dim(total, index, axis, False, allow_negative_indices=False)


def far_swap(send, sums, bit):
    high = lax.reduce_precision(sums, 8, 7)
    rest = sums - high
    middle = lax.reduce_precision(rest, 8, 7)
    parts = [part.astype(bf16) for part in (high, middle, rest - middle)]
    rows = send.reshape(-1, 128)
    got = swap(jnp.concatenate([rows.astype(bf16)] + parts, axis=0), bit).astype(f32)
    cut, count = rows.shape[0], sums.shape[0]
    other = [got[cut + i * count : cut + (i + 1) * count] for i in range(3)]
    return got[:cut].reshape(send.shape), sums + (other[0] + (other[1] + other[2]))


def far_halve(total, axis, bit, own, off, sums):
    keep = half(total, axis, own[bit])
    send = half(total, axis, off[bit])
    got, sums = far_swap(send, sums, bit)
    return keep + got, sums


def group_rows(lanes, first):
    channel = lax.broadcasted_iota(jnp.int32, (640, lanes), 0)
    start = (lax.broadcasted_iota(jnp.int32, (640, lanes), 1) - first) * CPG
    return jnp.where((channel >= start) & (channel < start + CPG), 1.0, 0.0).astype(f32)


def group_columns(rows, first):
    channel = lax.broadcasted_iota(jnp.int32, (rows, 640), 1)
    start = (lax.broadcasted_iota(jnp.int32, (rows, 640), 0) - first) * CPG
    return jnp.where((channel >= start) & (channel < start + CPG), 1.0, 0.0).astype(f32)


def exact(left, right):
    return jnp.dot(left, right, preferred_element_type=f32, precision=lax.Precision.HIGHEST)


def stats_kernel(
    bits_ref, upper_ref, lower_ref, head_ref, tail_ref, out_ref, first_ref, final_ref, means, seconds
):
    step, last = pl.program_id(0), pl.num_programs(0) - 1
    count = upper_ref.shape[0]
    @pl.when(step == 0)
    def _():
        first_ref[...] = head_ref[...]
        final_ref[...] = tail_ref[...]
        means[...] = jnp.zeros_like(means)
        seconds[...] = jnp.zeros_like(seconds)

    for part, ref in enumerate((upper_ref, lower_ref)):
        mean = jnp.sum(ref[...].astype(f32), axis=0, keepdims=True) * (1.0 / count)
        gap = ref[...].astype(f32) - mean
        means[pl.ds(2 * step + part, 1), :] = mean
        seconds[0:1, :] += jnp.sum(gap * gap, axis=0, keepdims=True)

    @pl.when(step == last)
    def _():
        blocks = BLOCKS
        total = jnp.sum(means[...], axis=0, keepdims=True) * (1.0 / blocks)
        to_groups, to_channels = group_rows(128, 0), group_columns(128, 0)
        eight = jnp.broadcast_to(total, (8, total.shape[1]))
        mean = exact(eight, to_groups) * (1.0 / CPG)
        gaps = means[0:blocks, :] - exact(mean, to_channels)[0:1]
        spread = seconds[0:1, :] + count * jnp.sum(gaps * gaps, axis=0, keepdims=True)
        second = exact(jnp.broadcast_to(spread, eight.shape), to_groups)
        both = jnp.concatenate([mean[0:1], second[0:1]], axis=0)
        out_ref[...] = jnp.broadcast_to(both[None], out_ref.shape)


BLOCKS = 6


def local_stats(bits, field, cot):
    rows, width = field.shape
    block = rows // BLOCKS
    field = pltpu.with_memory_space_constraint(field, pltpu.HBM)
    return pl.pallas_call(
        stats_kernel,
        grid=(BLOCKS // 2,),
        in_specs=[
            IN_SMEM,
            pl.BlockSpec((block, width), lambda i: (2 * i, 0)),
            pl.BlockSpec((block, width), lambda i: (2 * i + 1, 0)),
            pl.BlockSpec((FRAME, width), lambda i: (0, 0)),
            pl.BlockSpec((FRAME, width), lambda i: (rows // FRAME - 1, 0)),
        ],
        out_specs=[
            pl.BlockSpec((64, 2, 128), lambda i: (0, 0, 0)),
            pl.BlockSpec((FRAME, width), lambda i: (0, 0)),
            pl.BlockSpec((FRAME, width), lambda i: (0, 0)),
        ],
        out_shape=[
            jax.ShapeDtypeStruct((64, 2, 128), f32),
            pltpu.HBM((FRAME, width), bf16),
            pltpu.HBM((FRAME, width), bf16),
        ],
        scratch_shapes=[
            pltpu.VMEM((8, width), f32),
            pltpu.VMEM((8, width), f32),
        ],
        compiler_params=params(16),
        cost_estimate=cost(rows * width * 4, rows * width * 2),
    )(bits, field, field, *in_hbm(cot, cot))


def turn_kernel(field_ref, turned_ref):
    turned_ref[...] = field_ref[...].T


def turned(field):
    rows, width = field.shape
    return pl.pallas_call(
        turn_kernel,
        grid=(width // 128,),
        in_specs=[pl.BlockSpec((rows, 128), lambda i: (0, i))],
        out_specs=pl.BlockSpec((128, rows), lambda i: (i, 0)),
        out_shape=pltpu.HBM((width, rows), bf16),
        compiler_params=params(12),
        cost_estimate=cost(10**9, 10**7),
    )(field)


def sigmoid(values):
    return 0.5 * jnp.tanh(0.5 * values) + 0.5


def owners(chain):
    out = []
    for block in range(64):
        bit = {name: (block >> (5 - i)) & 1 for i, name in enumerate(OWNER)}
        if bit["z2"] == chain:
            place = 0
            for name in ORDERS[chain]:
                place = 2 * place + bit[name]
            out.append((block, place))
    return out


def segments(chain):
    parts = {}
    for start in range(240 * chain, 1920, 480):
        row = start
        while row < start + 240:
            tap, channel = divmod(row, 640)
            length = min(start + 240 - row, 640 - channel)
            parts.setdefault(tap, []).append((channel, length))
            row += length
    out, at = [], 0
    for tap in sorted(parts):
        out.append((tap, tuple(parts[tap]), at))
        at += sum(length for _, length in parts[tap])
    return out


def add_taps(chain, acc, act_ref, cot_ref, j):
    lanes = slice(CHUNK * j, CHUNK * j + CHUNK)
    for tap, parts, at in segments(chain):
        start = FRAME * (2 - tap) + CHUNK * j
        rows = [act_ref[channel : channel + length, lanes] for channel, length in parts]
        rows = rows[0] if len(rows) == 1 else jnp.concatenate(rows, axis=0)
        part = jnp.dot(rows, cot_ref[start : start + CHUNK, :], preferred_element_type=f32)
        if j == 0:
            acc[at : at + rows.shape[0], :] = part
        else:
            acc[at : at + rows.shape[0], :] += part


def pack_taps(chain, first, acc, send_ref, keep_ref):
    lane = lax.broadcasted_iota(jnp.int32, (32, 128), 1)
    low = lax.broadcasted_iota(jnp.int32, (16, 128), 1)
    for number, (_, place) in enumerate(owners(chain)):
        rows = slice(30 * number, 30 * number + 32)
        tile = [acc[rows, 128 * q : 128 * q + 128] for q in range(5)]
        main = [
            tile[0],
            jnp.where(lane < 96, pltpu.roll(tile[1], 96, 1), pltpu.roll(tile[2], 96, 1)),
            jnp.where(lane < 64, pltpu.roll(tile[2], 64, 1), pltpu.roll(tile[3], 64, 1)),
            jnp.where(lane < 32, pltpu.roll(tile[3], 32, 1), pltpu.roll(tile[4], 32, 1)),
        ]
        rest = [(tile[1], 0), (tile[2], 32), (tile[3], 64), (tile[4], 96)]
        last = []
        for core in range(2):
            pieces = [rest[core], rest[core + 2]]
            row16 = None
            for slot in range(4):
                source, at = pieces[slot % 2]
                part = source[16 * (slot // 2) : 16 * (slot // 2) + 16]
                shift = (32 * slot - at) % 128
                part = part if shift == 0 else pltpu.roll(part, shift, 1)
                row16 = part if row16 is None else jnp.where(low < 32 * slot, row16, part)
            last.append(row16)
        for at, zero, one in ((0, main[0], main[1]), (32, main[2], main[3]), (64, last[0], last[1])):
            span = slice(at, at + zero.shape[0])
            keep_ref[place, span] = jnp.where(first, zero, one)
            send_ref[place, span] = jnp.where(first, one, zero).astype(bf16)


def taps_a_kernel(
    core_ref, stats_ref, gain_ref, field_ref, before_ref, cot_ref, after_ref,
    coef_ref, act_ref, padded_ref, send_ref, keep_ref, acc, wide, field, sems,
):
    width, rows = field_ref.shape
    chunks = rows // CHUNK
    pieces = []
    for j in range(chunks):
        lanes = pl.ds(CHUNK * j, CHUNK)
        pieces.append((field_ref.at[:, lanes], field.at[:, lanes]))
    pieces.append((before_ref, padded_ref.at[pl.ds(0, FRAME)]))
    for t in range(rows // FRAME):
        pieces.append(
            (cot_ref.at[pl.ds(FRAME * t, FRAME)], padded_ref.at[pl.ds(FRAME * (t + 1), FRAME)])
        )
    pieces.append((after_ref, padded_ref.at[pl.ds(FRAME + rows, FRAME)]))
    copies = [pltpu.make_async_copy(*piece, sems.at[q]) for q, piece in enumerate(pieces)]
    for copy in copies:
        copy.start()
    total = jnp.sum(stats_ref[...], axis=0)
    mean = total[0:1] * (1.0 / 64)
    gaps = stats_ref[...] - mean[None]
    squares = jnp.sum(gaps * gaps, axis=0)[0:1]
    second = total[1:2] + squares * (CHAN_TOTAL // 64)
    both = jnp.concatenate([mean, second, jnp.zeros((6, 128), f32)], axis=0)
    spread = exact(both, group_columns(128, 0))
    mean, gamma, beta = spread[0:1], gain_ref[0:1, :], gain_ref[1:2, :]
    inv = lax.rsqrt(spread[1:2] * (1.0 / CHAN_TOTAL) + 1e-05)
    coef_ref[...] = jnp.concatenate([mean, inv, gamma, beta, jnp.zeros((4, width), f32)], axis=0)
    coef = jnp.concatenate([mean, inv * gamma, beta, jnp.zeros((5, width), f32)], axis=0).T
    for q in range(3):
        wide[q] = jnp.broadcast_to(coef[:, q : q + 1], (width, 128))

    def activate(j):
        copies[j].wait()
        for at in range(CHUNK * j, CHUNK * j + CHUNK, 128):
            lanes = slice(at, at + 128)
            normed = (field[:, lanes].astype(f32) - wide[0]) * wide[1] + wide[2]
            act_ref[:, lanes] = (normed * sigmoid(normed)).astype(bf16)

    activate(0)
    arrived = chunks
    for j in range(chunks):
        if j + 1 < chunks:
            activate(j + 1)
        needed = chunks + (2 * FRAME + CHUNK * (j + 1) - 1) // FRAME + 1
        for copy in copies[arrived:needed]:
            copy.wait()
        arrived = needed
        add_taps(0, acc, act_ref, padded_ref, j)
    for copy in copies[arrived:]:
        copy.wait()
    acc[960:, :] = jnp.zeros((8, width), f32)
    pack_taps(0, core_ref[0] == 0, acc, send_ref, keep_ref)


def taps_a(core, stats, gain, field_t, before, cot, after):
    width, rows = field_t.shape
    return pl.pallas_call(
        taps_a_kernel,
        in_specs=[IN_SMEM] + [IN_VMEM] * 2 + [ANYWHERE] * 4,
        out_specs=[IN_VMEM] * 5,
        out_shape=[
            jax.ShapeDtypeStruct((8, width), f32),
            vmem((width, rows), bf16),
            vmem((rows + 2 * FRAME, width), bf16),
            jax.ShapeDtypeStruct((32, 80, 128), bf16),
            vmem((32, 80, 128), f32),
        ],
        scratch_shapes=[
            pltpu.VMEM((968, width), f32),
            pltpu.VMEM((3, width, 128), f32),
            pltpu.VMEM((width, rows), bf16),
            pltpu.SemaphoreType.DMA((rows // CHUNK + rows // FRAME + 2,)),
        ],
        compiler_params=params(20),
        cost_estimate=cost(3 * width * rows * width, 10**7, width * rows),
    )(core, stats, gain, *in_hbm(field_t, before, cot, after))


def taps_b_kernel(core_ref, act_ref, padded_ref, send_ref, keep_ref, acc):
    width, rows = act_ref.shape
    for j in range(rows // CHUNK):
        add_taps(1, acc, act_ref, padded_ref, j)
    acc[960:, :] = jnp.zeros((8, width), f32)
    pack_taps(1, core_ref[0] == 0, acc, send_ref, keep_ref)


def taps_b(core, act, padded):
    width, rows = act.shape
    return pl.pallas_call(
        taps_b_kernel,
        in_specs=[IN_SMEM, IN_VMEM, IN_VMEM],
        out_specs=[IN_VMEM] * 2,
        out_shape=[
            jax.ShapeDtypeStruct((32, 80, 128), bf16),
            vmem((32, 80, 128), f32),
        ],
        scratch_shapes=[pltpu.VMEM((968, width), f32)],
        compiler_params=params(16),
        cost_estimate=cost(3 * width * rows * width, 10**7),
    )(core, act, padded)


def merge_kernel(slots, terms, bits_ref, *refs):
    count = len(slots)
    ins, sum_refs, outs = refs[: 2 * count], refs[2 * count : 2 * count + terms], refs[2 * count + terms :]
    for q, slot in enumerate(slots):
        kept_ref, got_ref = ins[2 * q : 2 * q + 2]
        keep_ref, send_ref = outs[2 * q : 2 * q + 2]
        size = keep_ref.shape[0]
        mine, other = pl.ds(bits_ref[slot] * size, size), pl.ds((1 - bits_ref[slot]) * size, size)
        keep_ref[...] = kept_ref[mine] + got_ref[mine].astype(f32)
        send_ref[...] = (kept_ref[other] + got_ref[other].astype(f32)).astype(bf16)
    sums_ref = outs[2 * count]
    if terms == 1:
        sums_ref[...] = sum_refs[0][...]
    else:
        every = lax.broadcasted_iota(jnp.int32, sums_ref.shape, 0) < 15
        here, core, there, both = (ref[...] for ref in sum_refs)
        sums_ref[...] = (here + jnp.where(every, core, 0.0)) + (there + jnp.where(every, both, 0.0))


def merge(bits, chains, sums):
    shapes, args = [], []
    for _, kept, got in chains:
        half_shape = (kept.shape[0] // 2,) + kept.shape[1:]
        shapes += [vmem(half_shape, f32), jax.ShapeDtypeStruct(half_shape, bf16)]
        args += [kept, got]
    shapes.append(jax.ShapeDtypeStruct(sums[0].shape, f32))
    args += sums
    slots = [list(BIT).index(bit) for bit, _, _ in chains]
    out = pl.pallas_call(
        functools.partial(merge_kernel, slots, len(sums)),
        in_specs=[IN_SMEM] + [IN_VMEM] * len(args),
        out_specs=[IN_VMEM] * len(shapes),
        out_shape=shapes,
        compiler_params=params(12),
        cost_estimate=cost(10**5, 10**5),
    )(bits, *args)
    return [(out[2 * q], out[2 * q + 1]) for q in range(len(chains))], out[-1]


def gradient_kernel(
    tie_ref, field_ref, prev_ref, cur_ref, next_ref, kernel_ref, coef_ref, held_ref,
    out_ref, held_out_ref, sums_ref, sums,
):
    step, last = pl.program_id(0), pl.num_programs(0) - 1
    mean, inv, gamma, beta = (coef_ref[q : q + 1, :] for q in range(4))

    @pl.when(step == 0)
    def _():
        sums[...] = held_ref[...]

    rows_by_rows = (((1,), (1,)), ((), ()))
    grad = lax.dot_general(next_ref[...], kernel_ref[0], rows_by_rows, preferred_element_type=f32)
    grad += lax.dot_general(cur_ref[...], kernel_ref[1], rows_by_rows, preferred_element_type=f32)
    grad += lax.dot_general(prev_ref[...], kernel_ref[2], rows_by_rows, preferred_element_type=f32)
    unit = (field_ref[...].astype(f32) - mean) * inv
    normed = unit * gamma + beta
    gate = sigmoid(normed)
    grad = grad * gate * (1.0 + normed * (1.0 - gate))
    out_ref[...] = grad
    sums[0:1, :] += jnp.sum(grad, axis=0, keepdims=True)
    sums[1:2, :] += jnp.sum(grad * unit, axis=0, keepdims=True)
    sums[2:3, :] += jnp.sum(cur_ref[...].astype(f32), axis=0, keepdims=True)

    @pl.when(step == last)
    def _():
        held_out_ref[...] = sums[...]
        for q in range(3):
            for at in range(5):
                sums_ref[5 * q + at : 5 * q + at + 1, :] = sums[q : q + 1, 128 * at : 128 * at + 128]
        weighted = sums[...] * gamma
        sums_ref[15:16, :] = (
            exact(weighted, group_rows(128, 0))[0:1] + exact(weighted, group_rows(128, GROUPS))[1:2]
        )


def gradient(tie, first, field, padded, kernel, coef, held):
    width = field.shape[1]

    def part(at):
        return pl.BlockSpec((FRAME, width), lambda i: (first + i + at, 0))

    top = pl.BlockSpec((8, width), lambda i: (0, 0))
    return pl.pallas_call(
        gradient_kernel,
        grid=(2,),
        in_specs=[
            ANYWHERE,
            part(0),
            part(0),
            part(1),
            part(2),
            pl.BlockSpec(kernel.shape, lambda i: (0, 0, 0)),
            top,
            top,
        ],
        out_specs=[
            pl.BlockSpec((FRAME, width), lambda i: (i, 0)),
            top,
            pl.BlockSpec((16, 128), lambda i: (0, 0)),
        ],
        out_shape=[
            vmem((2 * FRAME, width), f32),
            jax.ShapeDtypeStruct((8, width), f32),
            jax.ShapeDtypeStruct((16, 128), f32),
        ],
        scratch_shapes=[pltpu.VMEM((8, width), f32)],
        compiler_params=params(16),
        cost_estimate=cost(1, 1),
    )(tie, field, padded, padded, padded, kernel, coef, held)


def result_kernel(cot_ref, early_ref, late_ref, field_ref, coef_ref, sums_ref, out_ref, means):
    @pl.when(pl.program_id(0) == 0)
    def _():
        grouped = jnp.broadcast_to(sums_ref[15:16, :], (8, 128)) * (1.0 / CHAN_TOTAL)
        means[0:1, :] = exact(grouped, group_columns(128, 0))[0:1]
        means[1:2, :] = exact(grouped, group_columns(128, GROUPS))[0:1]

    mean, inv, gamma = (coef_ref[q : q + 1, :] for q in range(3))
    unit = (field_ref[...].astype(f32) - mean) * inv
    early = 2 * pl.program_id(0) < pl.num_programs(0)
    for when, grad_ref in ((early, early_ref), (jnp.logical_not(early), late_ref)):

        @pl.when(when)
        def _():
            out_ref[...] = (
                cot_ref[...].astype(f32)
                + inv * (gamma * grad_ref[...] - means[0:1, :] - unit * means[1:2, :])
            ).astype(bf16)


def grad_of_field(cot, early, late, field, coef, sums, block=288):
    rows, width = field.shape
    tile = pl.BlockSpec((block, width), lambda i: (i, 0))
    half_steps = rows // block // 2
    return pl.pallas_call(
        result_kernel,
        grid=(rows // block,),
        in_specs=[
            tile,
            pl.BlockSpec((block, width), lambda i: (jnp.minimum(i, half_steps - 1), 0)),
            pl.BlockSpec((block, width), lambda i: (jnp.maximum(i - half_steps, 0), 0)),
            tile,
            pl.BlockSpec((8, width), lambda i: (0, 0)),
            pl.BlockSpec((16, 128), lambda i: (0, 0)),
        ],
        out_specs=tile,
        out_shape=jax.ShapeDtypeStruct((rows, width), bf16),
        scratch_shapes=[pltpu.VMEM((8, width), f32)],
        compiler_params=params(12),
        cost_estimate=cost(rows * width * 9, rows * width * 10),
    )(cot, early, late, field, coef, sums)


def per_device(field, cotangent, gamma, beta, kernel):
    _, frames, rows, cells, width = field.shape
    loss_scale = 1.0 / math.sqrt(4 * 128 * 18 * 64)
    place = lax.axis_index(AXES)
    own = {name: (place >> bit) & 1 for name, bit in BIT.items()}
    off = {name: 1 - bit for name, bit in own.items()}
    bits = jnp.stack(list(own.values()) + list(off.values())).astype(jnp.int32)
    core = own["core"].astype(jnp.int32).reshape(1)
    gain = jnp.concatenate([gamma[None], beta[None], jnp.zeros((6, width), f32)], axis=0)

    flat, cot = field.reshape(-1, width), cotangent.reshape(-1, width)
    stats, first, final = local_stats(bits, flat, cot)
    up = [(i, i + 1) for i in range(31)]
    before = lax.ppermute(final, "tm", up)
    after = lax.ppermute(first, "tm", [(j, i) for i, j in up])
    stats = lax.all_to_all(stats, ("tm", "height"), 0, 0)
    field_t = turned(flat)

    coef, act_t, padded, send_a, keep_a = taps_a(core, stats, gain, field_t, before, cot, after)
    got_a = swap(send_a, "core")
    send_b, keep_b = taps_b(core, act_t, padded)
    got_b = swap(send_b, "core")
    none = jnp.zeros((8, width), f32)
    grad_early, held, _ = gradient(keep_b, 0, flat, padded, kernel, coef, none)
    kept, got = [keep_a, keep_b], [got_a, got_b]
    sums = [held]
    for step in range(3):
        merged, sums = merge(bits, [(ORDERS[q][step], kept[q], got[q]) for q in range(2)], sums)
        kept = [merged[q][0] for q in range(2)]
        got = [
            lax.ppermute(merged[q][1], AXES, neighbours(NEAR[ORDERS[q][step]])) for q in range(2)
        ]
        if step == 0:
            grad_late, _, sums = gradient(kept[0], 2, flat, padded, kernel, coef, sums)
            sums = [sums]
        elif step == 1:
            sums = [sums, swap(sums, "core"), swap(sums, "z0"), swap(sums, "core", "z0")]
        else:
            sums = (sums + swap(sums, "x0")) + (swap(sums, "yl") + swap(sums, "x0", "yl"))
    taps = jnp.stack([kept[q] + got[q].astype(f32) for q in range(2)])
    taps = taps.reshape(2, 2, 2, 80, 128)
    taps, sums = far_halve(taps, 2, "z1", own, off, sums)
    taps, sums = far_halve(taps, 1, "x1", own, off, sums)
    taps, sums = far_halve(taps, 0, "z2", own, off, sums)
    field_grad = grad_of_field(cot, grad_early, grad_late, flat, coef, sums)

    got, sums = far_swap(taps, sums, "yh")
    taps = taps + got
    main = half(taps[:64].reshape(2, 32, 128), 0, own["yh"])
    rest = half(taps[64:].reshape(16, 2, 2, 32), 2, own["yh"])
    rest = jnp.concatenate([rest[:, 0], rest[:, 1]], axis=0)
    kernel_grad = jnp.concatenate([main, rest], axis=1)[:30] * loss_scale
    channel_grads = sums[:15].reshape(3, width) * loss_scale
    return (field_grad.reshape(field.shape), kernel_grad, channel_grads)


def solution(mesh):
    spread = P("dp", "tm", "height", None, None)
    return jax.shard_map(
        per_device,
        mesh=mesh,
        in_specs=(spread, spread, P(), P(), P()),
        out_specs=(spread, P(("tm", "height"), "dp"), P()),
        check_vma=False,
    )
```

profile of v0, /device:TPU:2, one launch (start us, length us, event | category | flops | bytes accessed | tf_op | source)
XLA Modules:
  0.0 117.1 jit_solution(9138423832570767555)
XLA Ops:
  0.8 6.4 %shard_map.76 = (f32[64,2,128]{2,1,0:T(2,128)}, bf16[576,640]{1,0:T(8,128)(2,1)}, bf16[576,640]{1,0:T(8,128)(2,1)}) custom-call(s32[16]{0:T(128)S(1)} %stack.73.bits_ref, bf16[2304,640]{1,0:T(8,128)(2,1)} %bitcast.55, bf16[2304,640]{1,0:T(8,128)(2,1)} %bitcast.56, bf16[2304,640]{1,0:T(8,128)(2,1)} %bitcast.61, bf16[2304,640]{1,0:T(8,128)(2,1)} %bitcast.62), custom_call_target="tpu_custom_call" | custom-call | flops 5898240 | bytes 2949120 | tf_op jit(solution)/shard_map/pallas_call | solution.py:153
  7.2 3.8 %collective-permute-start = (bf16[576,640]{1,0:T(8,128)(2,1)}, bf16[576,640]{1,0:T(8,128)(2,1)}, u32[]{:S(2)}, u32[]{:S(2)}) collective-permute-start(bf16[576,640]{1,0:T(8,128)(2,1)} %get-tuple-element.33), channel_id=1, source_target_pairs={{0,2},{2,4},{4,6},{6,8},{8,10},{10,12},{12,14},{14,16},{16,18},{18... | collective-permute-start | bytes 2211848 | tf_op jit(solution)/shard_map/ppermute | solution.py:545
  11.0 5.8 %collective-permute-start.1 = (bf16[576,640]{1,0:T(8,128)(2,1)}, bf16[576,640]{1,0:T(8,128)(2,1)}, u32[]{:S(2)}, u32[]{:S(2)}) collective-permute-start(bf16[576,640]{1,0:T(8,128)(2,1)} %get-tuple-element.34), channel_id=1, source_target_pairs={{2,0},{4,2},{6,4},{8,6},{10,8},{12,10},{14,12},{16,14},{18,16},{20... | collective-permute-start | bytes 2211848 | tf_op jit(solution)/shard_map/ppermute | solution.py:546
  16.8 10.4 %all-to-all-start = ((f32[64,2,128]{2,1,0:T(2,128)}), f32[64,2,128]{2,1,0:T(2,128)S(1)}, u32[]{:S(2)}, u32[]{:S(2)}) async-start(f32[64,2,128]{2,1,0:T(2,128)} %get-tuple-element.32), calls=%async_computation | async-start | bytes 131072 | tf_op jit(solution)/shard_map/all_to_all | solution.py:547
  27.5 3.4 %shard_map.77.field_ref = bf16[640,2304]{1,0:T(8,128)(2,1)} custom-call(bf16[2304,640]{1,0:T(8,128)(2,1)S(1)} %bitcast.57), custom_call_target="tpu_custom_call" | custom-call | flops 1000000000 | bytes 10000000 | tf_op jit(solution)/shard_map/pallas_call | solution.py:188
  30.9 7.5 %all-to-all-done.stats_ref = f32[64,2,128]{2,1,0:T(2,128)S(1)} async-done(((f32[64,2,128]{2,1,0:T(2,128)}), f32[64,2,128]{2,1,0:T(2,128)S(1)}, u32[]{:S(2)}, u32[]{:S(2)}) %all-to-all-start) | async-done | bytes 65568 | tf_op jit(solution)/shard_map/all_to_all | solution.py:547
  38.4 8.5 %shard_map.78 = (f32[8,640]{1,0:T(8,128)S(1)}, bf16[640,2304]{1,0:T(8,128)(2,1)S(1)}, bf16[3456,640]{1,0:T(8,128)(2,1)S(1)}, bf16[32,80,128]{2,1,0:T(8,128)(2,1)S(1)}, f32[32,80,128]{2,1,0:T(8,128)S(1)}) custom-call(s32[1]{0:T(128)} %bitcast.1.core_ref, f32[64,2,128]{2,1,0:T(2,128)S(1)} %all-to-all-done.stats_ref, ...), custom_call_target="tpu_custom_call" | custom-call | flops 2831155200 | bytes 10000000 | tf_op jit(solution)/shard_map/pallas_call | solution.py:332
  46.9 4.2 %shard_map.79 = (bf16[32,80,128]{2,1,0:T(8,128)(2,1)S(1)}, f32[32,80,128]{2,1,0:T(8,128)S(1)}) custom-call(s32[1]{0:T(128)} %bitcast.1.core_ref, bf16[640,2304]{1,0:T(8,128)(2,1)S(1)} %get-tuple-element.35.act_ref, bf16[3456,640]{1,0:T(8,128)(2,1)S(1)} %get-tuple-element.36.padded_ref.prev_ref.cur_ref.next_ref), custom_call_target="tpu_custom_call" | custom-call | flops 2831155200 | bytes 10000000 | tf_op jit(solution)/shard_map/pallas_call | solution.py:364
  51.8 6.5 %shard_map.80 = (f32[1152,640]{1,0:T(8,128)S(1)}, f32[8,640]{1,0:T(8,128)S(1)}, f32[16,128]{1,0:T(8,128)}) custom-call(f32[32,80,128]{2,1,0:T(8,128)S(1)} %get-tuple-element.37.tie_ref.refs_2_, bf16[2304,640]{1,0:T(8,128)(2,1)S(1)} %bitcast.58, bf16[3456,640]{1,0:T(8,128)(2,1)S(1)} %get-tuple-element.36.padded_ref.prev_ref.cur_ref.next_ref, ...), custom_call_target="tpu_custom_call" | custom-call | flops 1 | bytes 1 | tf_op jit(solution)/shard_map/pallas_call | solution.py:460
  59.1 3.6 %collective-permute-start.4 = (bf16[16,80,128]{2,1,0:T(8,128)(2,1)S(1)}, bf16[16,80,128]{2,1,0:T(8,128)(2,1)S(1)}, u32[]{:S(2)}, u32[]{:S(2)}) collective-permute-start(bf16[16,80,128]{2,1,0:T(8,128)(2,1)S(1)} %get-tuple-element.47), channel_id=1, source_target_pairs={{0,2},{1,3},{2,0},{3,1},{4,6},{5,7},{6,4},{7,5},{8,10},{9,11},{10,... | collective-permute-start | bytes 983048 | tf_op jit(solution)/shard_map/ppermute | solution.py:562
  63.3 6.5 %shard_map.82 = (f32[1152,640]{1,0:T(8,128)S(1)}, f32[8,640]{1,0:T(8,128)}, f32[16,128]{1,0:T(8,128)S(1)}) custom-call(f32[16,80,128]{2,1,0:T(8,128)S(1)} %get-tuple-element.44.tie_ref.refs_0_, bf16[2304,640]{1,0:T(8,128)(2,1)S(1)} %bitcast.59, bf16[3456,640]{1,0:T(8,128)(2,1)S(1)} %get-tuple-element.36.padded_ref.prev_ref.cur_ref.next_ref, ...), custom_call_target="tpu_custom_call" | custom-call | flops 1 | bytes 1 | tf_op jit(solution)/shard_map/pallas_call | solution.py:460
  70.5 1.5 %collective-permute-start.6 = (bf16[8,80,128]{2,1,0:T(8,128)(2,1)S(1)}, bf16[8,80,128]{2,1,0:T(8,128)(2,1)S(1)}, u32[]{:S(2)}, u32[]{:S(2)}) collective-permute-start(bf16[8,80,128]{2,1,0:T(8,128)(2,1)S(1)} %get-tuple-element.52), channel_id=1, source_target_pairs={{0,16},{1,17},{2,18},{3,19},{4,20},{5,21},{6,22},{7,23},{8,24},{9,... | collective-permute-start | bytes 491528 | tf_op jit(solution)/shard_map/ppermute | solution.py:562
  72.1 1.6 %collective-permute-start.10 = (f32[16,128]{1,0:T(8,128)S(1)}, f32[16,128]{1,0:T(8,128)S(1)}, u32[]{:S(2)}, u32[]{:S(2)}) collective-permute-start(f32[16,128]{1,0:T(8,128)S(1)} %get-tuple-element.55.refs_4_), channel_id=1, source_target_pairs={{0,66},{1,67},{2,64},{3,65},{4,70},{5,71},{6,68},{7,69},{8,74},{9,... | collective-permute-start | bytes 24584 | tf_op jit(solution)/shard_map/ppermute | solution.py:72
  75.2 2.6 %collective-permute-done.9.refs_6_ = f32[16,128]{1,0:T(8,128)S(1)} collective-permute-done((f32[16,128]{1,0:T(8,128)S(1)}, f32[16,128]{1,0:T(8,128)S(1)}, u32[]{:S(2)}, u32[]{:S(2)}) %collective-permute-start.9) | collective-permute-done | bytes 8224 | tf_op jit(solution)/shard_map/ppermute | solution.py:72
  78.4 1.6 %collective-permute-start.11 = (f32[16,128]{1,0:T(8,128)S(1)}, f32[16,128]{1,0:T(8,128)S(1)}, u32[]{:S(2)}, u32[]{:S(2)}) collective-permute-start(f32[16,128]{1,0:T(8,128)S(1)} %get-tuple-element.56), channel_id=1, source_target_pairs={{0,16},{1,17},{2,18},{3,19},{4,20},{5,21},{6,22},{7,23},{8,24},{9,... | collective-permute-start | bytes 24584 | tf_op jit(solution)/shard_map/ppermute | solution.py:72
  80.6 1.4 %collective-permute-start.13 = (f32[16,128]{1,0:T(8,128)S(1)}, f32[16,128]{1,0:T(8,128)S(1)}, u32[]{:S(2)}, u32[]{:S(2)}) collective-permute-start(f32[16,128]{1,0:T(8,128)S(1)} %get-tuple-element.56), channel_id=1, source_target_pairs={{0,17},{1,16},{2,19},{3,18},{4,21},{5,20},{6,23},{7,22},{8,25},{9,... | collective-permute-start | bytes 24584 | tf_op jit(solution)/shard_map/ppermute | solution.py:72
  82.0 1.5 %collective-permute-start.15 = (bf16[4,80,128]{2,1,0:T(8,128)(2,1)S(1)}, bf16[4,80,128]{2,1,0:T(8,128)(2,1)S(1)}, u32[]{:S(2)}, u32[]{:S(2)}) collective-permute-start(bf16[4,80,128]{2,1,0:T(8,128)(2,1)S(1)} %get-tuple-element.60), channel_id=1, source_target_pairs={{0,16},{1,17},{2,18},{3,19},{4,20},{5,21},{6,22},{7,23},{8,24},{9,... | collective-permute-start | bytes 245768 | tf_op jit(solution)/shard_map/ppermute | solution.py:562
  86.5 1.5 %collective-permute-done.14 = bf16[4,80,128]{2,1,0:T(8,128)(2,1)S(1)} collective-permute-done((bf16[4,80,128]{2,1,0:T(8,128)(2,1)S(1)}, bf16[4,80,128]{2,1,0:T(8,128)(2,1)S(1)}, u32[]{:S(2)}, u32[]{:S(2)}) %collective-permute-start.14) | collective-permute-done | bytes 81952 | tf_op jit(solution)/shard_map/ppermute | solution.py:562
  88.0 2.0 %collective-permute-start.16 = (bf16[368,128]{1,0:T(8,128)(2,1)S(1)}, bf16[368,128]{1,0:T(8,128)(2,1)S(1)}, u32[]{:S(2)}, u32[]{:S(2)}) collective-permute-start(bf16[368,128]{1,0:T(8,128)(2,1)S(1)} %pad_maximum_fusion), channel_id=1, source_target_pairs={{0,4},{1,5},{2,6},{3,7},{4,0},{5,1},{6,2},{7,3},{8,12},{9,13},{10,... | collective-permute-start | bytes 282632 | tf_op jit(solution)/shard_map/ppermute | solution.py:72
  90.0 4.4 %collective-permute-done.16 = bf16[368,128]{1,0:T(8,128)(2,1)S(1)} collective-permute-done((bf16[368,128]{1,0:T(8,128)(2,1)S(1)}, bf16[368,128]{1,0:T(8,128)(2,1)S(1)}, u32[]{:S(2)}, u32[]{:S(2)}) %collective-permute-start.16) | collective-permute-done | bytes 94240 | tf_op jit(solution)/shard_map/ppermute | solution.py:72
  95.6 4.5 %collective-permute-done.17 = bf16[208,128]{1,0:T(8,128)(2,1)S(1)} collective-permute-done((bf16[208,128]{1,0:T(8,128)(2,1)S(1)}, bf16[208,128]{1,0:T(8,128)(2,1)S(1)}, u32[]{:S(2)}, u32[]{:S(2)}) %collective-permute-start.17) | collective-permute-done | bytes 53280 | tf_op jit(solution)/shard_map/ppermute | solution.py:72
  101.3 6.9 %collective-permute-done.18 = bf16[128,128]{1,0:T(8,128)(2,1)S(1)} collective-permute-done((bf16[128,128]{1,0:T(8,128)(2,1)S(1)}, bf16[128,128]{1,0:T(8,128)(2,1)S(1)}, u32[]{:S(2)}, u32[]{:S(2)}) %collective-permute-start.18) | collective-permute-done | bytes 32800 | tf_op jit(solution)/shard_map/ppermute | solution.py:72
  108.3 2.1 %collective-permute-start.19 = (bf16[128,128]{1,0:T(8,128)(2,1)S(1)}, bf16[128,128]{1,0:T(8,128)(2,1)S(1)}, u32[]{:S(2)}, u32[]{:S(2)}) collective-permute-start(bf16[128,128]{1,0:T(8,128)(2,1)S(1)} %pad_maximum_fusion.5), channel_id=1, source_target_pairs={{0,128},{1,129},{2,130},{3,131},{4,132},{5,133},{6,134},{7,135},{8... | collective-permute-start | bytes 98312 | tf_op jit(solution)/shard_map/ppermute | solution.py:72
  110.4 5.3 %shard_map.85 = bf16[2304,640]{1,0:T(8,128)(2,1)} custom-call(bf16[2304,640]{1,0:T(8,128)(2,1)S(1)} %bitcast.64, f32[1152,640]{1,0:T(8,128)S(1)} %get-tuple-element.39.early_ref, f32[1152,640]{1,0:T(8,128)S(1)} %get-tuple-element.46.late_ref, bf16[2304,640]{1,0:T(8,128)(2,1)S(1)} %bitcast.60, f32[8,640]{1,0:T(8,128)S(1)} %get-tuple-element.38.coef_ref, ...), custom_call_target="tpu_custom_call" | custom-call | flops 13271040 | bytes 14745600 | tf_op jit(solution)/shard_map/pallas_call | solution.py:513
  (83 shorter events, 12.6 us)
Async XLA Ops:
  0.8 26.6 %copy-start.4 = (f32[640]{0:T(1024)S(1)}, f32[640]{0:T(1024)}, u32[]{:S(2)}) copy-start(f32[640]{0:T(1024)} %param.8) | copy-start | bytes 7684
  0.8 26.7 %copy-start = (bf16[1,4,9,64,640]{4,3,2,1,0:T(8,128)(2,1)S(1)}, bf16[1,4,9,64,640]{4,3,2,1,0:T(8,128)(2,1)}, u32[]{:S(2)}) copy-start(bf16[1,4,9,64,640]{4,3,2,1,0:T(8,128)(2,1)} %param.5) | copy-start | bytes 8847364
  7.2 31.2 %collective-permute-start = (bf16[576,640]{1,0:T(8,128)(2,1)}, bf16[576,640]{1,0:T(8,128)(2,1)}, u32[]{:S(2)}, u32[]{:S(2)}) collective-permute-start(bf16[576,640]{1,0:T(8,128)(2,1)} %get-tuple-element.33), channel_id=1, source_target_pairs={{0,2},{2,4},{4,6},{6,8},{8,10},{10,12},{12,14},{14,16},{16,18},{18... | collective-permute-start | bytes 2211848 | tf_op jit(solution)/shard_map/ppermute | solution.py:545
  11.0 27.4 %collective-permute-start.1 = (bf16[576,640]{1,0:T(8,128)(2,1)}, bf16[576,640]{1,0:T(8,128)(2,1)}, u32[]{:S(2)}, u32[]{:S(2)}) collective-permute-start(bf16[576,640]{1,0:T(8,128)(2,1)} %get-tuple-element.34), channel_id=1, source_target_pairs={{2,0},{4,2},{6,4},{8,6},{10,8},{12,10},{14,12},{16,14},{18,16},{20... | collective-permute-start | bytes 2211848 | tf_op jit(solution)/shard_map/ppermute | solution.py:546
  16.8 21.5 %all-to-all-start = ((f32[64,2,128]{2,1,0:T(2,128)}), f32[64,2,128]{2,1,0:T(2,128)S(1)}, u32[]{:S(2)}, u32[]{:S(2)}) async-start(f32[64,2,128]{2,1,0:T(2,128)} %get-tuple-element.32), calls=%async_computation | async-start | bytes 131072 | tf_op jit(solution)/shard_map/all_to_all | solution.py:547
  51.2 7.1 %collective-permute-start.3 = (bf16[32,80,128]{2,1,0:T(8,128)(2,1)S(1)}, bf16[32,80,128]{2,1,0:T(8,128)(2,1)S(1)}, u32[]{:S(2)}, u32[]{:S(2)}) collective-permute-start(bf16[32,80,128]{2,1,0:T(8,128)(2,1)S(1)} %get-tuple-element.42), channel_id=1, source_target_pairs={{0,64},{1,65},{2,66},{3,67},{4,68},{5,69},{6,70},{7,71},{8,72},{9,... | collective-permute-start | bytes 1966088 | tf_op jit(solution)/shard_map/ppermute | solution.py:72
  51.3 7.0 %collective-permute-start.2 = (bf16[32,80,128]{2,1,0:T(8,128)(2,1)S(1)}, bf16[32,80,128]{2,1,0:T(8,128)(2,1)S(1)}, u32[]{:S(2)}, u32[]{:S(2)}) collective-permute-start(bf16[32,80,128]{2,1,0:T(8,128)(2,1)S(1)} %get-tuple-element.41), channel_id=1, source_target_pairs={{0,64},{1,65},{2,66},{3,67},{4,68},{5,69},{6,70},{7,71},{8,72},{9,... | collective-permute-start | bytes 1966088 | tf_op jit(solution)/shard_map/ppermute | solution.py:72
  59.1 10.7 %collective-permute-start.4 = (bf16[16,80,128]{2,1,0:T(8,128)(2,1)S(1)}, bf16[16,80,128]{2,1,0:T(8,128)(2,1)S(1)}, u32[]{:S(2)}, u32[]{:S(2)}) collective-permute-start(bf16[16,80,128]{2,1,0:T(8,128)(2,1)S(1)} %get-tuple-element.47), channel_id=1, source_target_pairs={{0,2},{1,3},{2,0},{3,1},{4,6},{5,7},{6,4},{7,5},{8,10},{9,11},{10,... | collective-permute-start | bytes 983048 | tf_op jit(solution)/shard_map/ppermute | solution.py:562
  62.7 7.1 %collective-permute-start.5 = (bf16[16,80,128]{2,1,0:T(8,128)(2,1)S(1)}, bf16[16,80,128]{2,1,0:T(8,128)(2,1)S(1)}, u32[]{:S(2)}, u32[]{:S(2)}) collective-permute-start(bf16[16,80,128]{2,1,0:T(8,128)(2,1)S(1)} %get-tuple-element.49), channel_id=1, source_target_pairs={{0,1},{1,0},{2,3},{3,2},{4,5},{5,4},{6,7},{7,6},{8,9},{9,8},{10,11... | collective-permute-start | bytes 983048 | tf_op jit(solution)/shard_map/ppermute | solution.py:562
  70.5 39.9 %copy-start.1 = (bf16[1,4,9,64,640]{4,3,2,1,0:T(8,128)(2,1)S(1)}, bf16[1,4,9,64,640]{4,3,2,1,0:T(8,128)(2,1)}, u32[]{:S(2)}) copy-start(bf16[1,4,9,64,640]{4,3,2,1,0:T(8,128)(2,1)} %param.6) | copy-start | bytes 8847364
  70.5 7.3 %collective-permute-start.6 = (bf16[8,80,128]{2,1,0:T(8,128)(2,1)S(1)}, bf16[8,80,128]{2,1,0:T(8,128)(2,1)S(1)}, u32[]{:S(2)}, u32[]{:S(2)}) collective-permute-start(bf16[8,80,128]{2,1,0:T(8,128)(2,1)S(1)} %get-tuple-element.52), channel_id=1, source_target_pairs={{0,16},{1,17},{2,18},{3,19},{4,20},{5,21},{6,22},{7,23},{8,24},{9,... | collective-permute-start | bytes 491528 | tf_op jit(solution)/shard_map/ppermute | solution.py:562
  72.0 5.8 %collective-permute-start.7 = (bf16[8,80,128]{2,1,0:T(8,128)(2,1)S(1)}, bf16[8,80,128]{2,1,0:T(8,128)(2,1)S(1)}, u32[]{:S(2)}, u32[]{:S(2)}) collective-permute-start(bf16[8,80,128]{2,1,0:T(8,128)(2,1)S(1)} %get-tuple-element.54), channel_id=1, source_target_pairs={{0,2},{1,3},{2,0},{3,1},{4,6},{5,7},{6,4},{7,5},{8,10},{9,11},{10,... | collective-permute-start | bytes 491528 | tf_op jit(solution)/shard_map/ppermute | solution.py:562
  72.1 3.1 %collective-permute-start.10 = (f32[16,128]{1,0:T(8,128)S(1)}, f32[16,128]{1,0:T(8,128)S(1)}, u32[]{:S(2)}, u32[]{:S(2)}) collective-permute-start(f32[16,128]{1,0:T(8,128)S(1)} %get-tuple-element.55.refs_4_), channel_id=1, source_target_pairs={{0,66},{1,67},{2,64},{3,65},{4,70},{5,71},{6,68},{7,69},{8,74},{9,... | collective-permute-start | bytes 24584 | tf_op jit(solution)/shard_map/ppermute | solution.py:72
  73.7 1.5 %collective-permute-start.8 = (f32[16,128]{1,0:T(8,128)S(1)}, f32[16,128]{1,0:T(8,128)S(1)}, u32[]{:S(2)}, u32[]{:S(2)}) collective-permute-start(f32[16,128]{1,0:T(8,128)S(1)} %get-tuple-element.55.refs_4_), channel_id=1, source_target_pairs={{0,64},{1,65},{2,66},{3,67},{4,68},{5,69},{6,70},{7,71},{8,72},{9,... | collective-permute-start | bytes 24584 | tf_op jit(solution)/shard_map/ppermute | solution.py:72
  74.1 3.7 %collective-permute-start.9 = (f32[16,128]{1,0:T(8,128)S(1)}, f32[16,128]{1,0:T(8,128)S(1)}, u32[]{:S(2)}, u32[]{:S(2)}) collective-permute-start(f32[16,128]{1,0:T(8,128)S(1)} %get-tuple-element.55.refs_4_), channel_id=1, source_target_pairs={{0,2},{1,3},{2,0},{3,1},{4,6},{5,7},{6,4},{7,5},{8,10},{9,11},{10,... | collective-permute-start | bytes 24584 | tf_op jit(solution)/shard_map/ppermute | solution.py:72
  78.4 5.7 %collective-permute-start.11 = (f32[16,128]{1,0:T(8,128)S(1)}, f32[16,128]{1,0:T(8,128)S(1)}, u32[]{:S(2)}, u32[]{:S(2)}) collective-permute-start(f32[16,128]{1,0:T(8,128)S(1)} %get-tuple-element.56), channel_id=1, source_target_pairs={{0,16},{1,17},{2,18},{3,19},{4,20},{5,21},{6,22},{7,23},{8,24},{9,... | collective-permute-start | bytes 24584 | tf_op jit(solution)/shard_map/ppermute | solution.py:72
  80.0 4.1 %collective-permute-start.12 = (f32[16,128]{1,0:T(8,128)S(1)}, f32[16,128]{1,0:T(8,128)S(1)}, u32[]{:S(2)}, u32[]{:S(2)}) collective-permute-start(f32[16,128]{1,0:T(8,128)S(1)} %get-tuple-element.56), channel_id=1, source_target_pairs={{0,1},{1,0},{2,3},{3,2},{4,5},{5,4},{6,7},{7,6},{8,9},{9,8},{10,11... | collective-permute-start | bytes 24584 | tf_op jit(solution)/shard_map/ppermute | solution.py:72
  80.6 4.5 %collective-permute-start.13 = (f32[16,128]{1,0:T(8,128)S(1)}, f32[16,128]{1,0:T(8,128)S(1)}, u32[]{:S(2)}, u32[]{:S(2)}) collective-permute-start(f32[16,128]{1,0:T(8,128)S(1)} %get-tuple-element.56), channel_id=1, source_target_pairs={{0,17},{1,16},{2,19},{3,18},{4,21},{5,20},{6,23},{7,22},{8,25},{9,... | collective-permute-start | bytes 24584 | tf_op jit(solution)/shard_map/ppermute | solution.py:72
  82.0 4.4 %collective-permute-start.15 = (bf16[4,80,128]{2,1,0:T(8,128)(2,1)S(1)}, bf16[4,80,128]{2,1,0:T(8,128)(2,1)S(1)}, u32[]{:S(2)}, u32[]{:S(2)}) collective-permute-start(bf16[4,80,128]{2,1,0:T(8,128)(2,1)S(1)} %get-tuple-element.60), channel_id=1, source_target_pairs={{0,16},{1,17},{2,18},{3,19},{4,20},{5,21},{6,22},{7,23},{8,24},{9,... | collective-permute-start | bytes 245768 | tf_op jit(solution)/shard_map/ppermute | solution.py:562
  83.5 4.4 %collective-permute-start.14 = (bf16[4,80,128]{2,1,0:T(8,128)(2,1)S(1)}, bf16[4,80,128]{2,1,0:T(8,128)(2,1)S(1)}, u32[]{:S(2)}, u32[]{:S(2)}) collective-permute-start(bf16[4,80,128]{2,1,0:T(8,128)(2,1)S(1)} %get-tuple-element.58), channel_id=1, source_target_pairs={{0,1},{1,0},{2,3},{3,2},{4,5},{5,4},{6,7},{7,6},{8,9},{9,8},{10,11... | collective-permute-start | bytes 245768 | tf_op jit(solution)/shard_map/ppermute | solution.py:562
  88.0 6.3 %collective-permute-start.16 = (bf16[368,128]{1,0:T(8,128)(2,1)S(1)}, bf16[368,128]{1,0:T(8,128)(2,1)S(1)}, u32[]{:S(2)}, u32[]{:S(2)}) collective-permute-start(bf16[368,128]{1,0:T(8,128)(2,1)S(1)} %pad_maximum_fusion), channel_id=1, source_target_pairs={{0,4},{1,5},{2,6},{3,7},{4,0},{5,1},{6,2},{7,3},{8,12},{9,13},{10,... | collective-permute-start | bytes 282632 | tf_op jit(solution)/shard_map/ppermute | solution.py:72
  94.4 5.7 %collective-permute-start.17 = (bf16[208,128]{1,0:T(8,128)(2,1)S(1)}, bf16[208,128]{1,0:T(8,128)(2,1)S(1)}, u32[]{:S(2)}, u32[]{:S(2)}) collective-permute-start(bf16[208,128]{1,0:T(8,128)(2,1)S(1)} %pad_maximum_fusion.1), channel_id=1, source_target_pairs={{0,32},{1,33},{2,34},{3,35},{4,36},{5,37},{6,38},{7,39},{8,40},{9,... | collective-permute-start | bytes 159752 | tf_op jit(solution)/shard_map/ppermute | solution.py:72
  100.3 7.9 %collective-permute-start.18 = (bf16[128,128]{1,0:T(8,128)(2,1)S(1)}, bf16[128,128]{1,0:T(8,128)(2,1)S(1)}, u32[]{:S(2)}, u32[]{:S(2)}) collective-permute-start(bf16[128,128]{1,0:T(8,128)(2,1)S(1)} %pad_maximum_fusion.4), channel_id=1, source_target_pairs={{0,8},{1,9},{2,10},{3,11},{4,12},{5,13},{6,14},{7,15},{8,0},{9,1},... | collective-permute-start | bytes 98312 | tf_op jit(solution)/shard_map/ppermute | solution.py:72
  108.3 7.4 %collective-permute-start.19 = (bf16[128,128]{1,0:T(8,128)(2,1)S(1)}, bf16[128,128]{1,0:T(8,128)(2,1)S(1)}, u32[]{:S(2)}, u32[]{:S(2)}) collective-permute-start(bf16[128,128]{1,0:T(8,128)(2,1)S(1)} %pad_maximum_fusion.5), channel_id=1, source_target_pairs={{0,128},{1,129},{2,130},{3,131},{4,132},{5,133},{6,134},{7,135},{8... | collective-permute-start | bytes 98312 | tf_op jit(solution)/shard_map/ppermute | solution.py:72
  (2 other events, 31.4 us)
where the time goes:
time: 118 us; the launch traced here: 117 us
  Pallas kernels  42.9 us (36%)
  starting transfers between devices  40.6 us (34%)
  waiting for transfers between devices  30.6 us (26%)
    ppermute x12, waiting for transfers between devices, swap(): return lax.ppermute(value, AXES, chosen)  20.4 us
    pallas_call x2, Pallas kernels, gradient(): pl.pallas_call(gradient_kernel, grid=(2,), in_specs=[ANYWHERE, part(0), p...  13 us
    ppermute x12, starting transfers between devices, swap(): return lax.ppermute(value, AXES, chosen)  12.6 us
    all_to_all x1, starting transfers between devices, per_device(): stats = lax.all_to_all(stats, ('tm', 'height'), 0, 0)  10.4 us
    pallas_call x1, Pallas kernels, taps_a(): pl.pallas_call(taps_a_kernel, in_specs=[IN_SMEM] + [IN_VMEM] * 2 + [ANYWH...  8.52 us
    ppermute x6, starting transfers between devices, per_device(): lax.ppermute(merged[q][1], AXES, neighbours(NEAR[ORDERS[q][step]]))  7.92 us
    all_to_all x1, waiting for transfers between devices, per_device(): stats = lax.all_to_all(stats, ('tm', 'height'), 0, 0)  7.48 us
    pallas_call x1, Pallas kernels, local_stats(): pl.pallas_call(stats_kernel, grid=(BLOCKS // 2,), in_specs=[IN_SMEM, pl.B...  6.38 us
  transfers between devices with their start and end apart: 21, of which 9 were waited for; matrix products, arithmetic and copies ran while one was open for 0% of the time, Pallas kernels for 19%

commit v1 on v0

--- a/solution.py
+++ b/solution.py
@@ -196,8 +196,32 @@
     )(field)
 
 
-def sigmoid(values):
-    return 0.5 * jnp.tanh(0.5 * values) + 0.5
+def grad_act_kernel(prev_ref, cur_ref, next_ref, kernel_ref, out_ref):
+    out_ref[...] = frame_grad_act(prev_ref[...], cur_ref[...], next_ref[...], kernel_ref)
+
+
+def frame_grad_act(before, here, after, kernel_ref):
+    rows_by_rows = (((1,), (1,)), ((), ()))
+    out = lax.dot_general(after, kernel_ref[0], rows_by_rows, preferred_element_type=f32)
+    out += lax.dot_general(here, kernel_ref[1], rows_by_rows, preferred_element_type=f32)
+    return out + lax.dot_general(before, kernel_ref[2], rows_by_rows, preferred_element_type=f32)
+
+
+def inner_grad_act(cot, kernel):
+    width = cot.shape[1]
+
+    def part(at):
+        return pl.BlockSpec((FRAME, width), lambda i: (i + at, 0))
+
+    return pl.pallas_call(
+        grad_act_kernel,
+        grid=(2,),
+        in_specs=[part(0), part(1), part(2), pl.BlockSpec(kernel.shape, lambda i: (0, 0, 0))],
+        out_specs=pl.BlockSpec((FRAME, width), lambda i: (i, 0)),
+        out_shape=pltpu.HBM((2 * FRAME, width), f32),
+        compiler_params=params(20),
+        cost_estimate=cost(10**9, 10**7),
+    )(*in_hbm(cot, cot, cot, kernel))
 
 
 def owners(chain):
@@ -272,7 +296,7 @@
 
 
 def taps_a_kernel(
-    core_ref, stats_ref, gain_ref, field_ref, before_ref, cot_ref, after_ref,
+    core_ref, stats_ref, gain_ref, field_ref, before_ref, cot_ref, after_ref, tie_ref,
     coef_ref, act_ref, padded_ref, send_ref, keep_ref, acc, wide, field, sems,
 ):
     width, rows = field_ref.shape
@@ -288,8 +312,7 @@
         )
     pieces.append((after_ref, padded_ref.at[pl.ds(FRAME + rows, FRAME)]))
     copies = [pltpu.make_async_copy(*piece, sems.at[q]) for q, piece in enumerate(pieces)]
-    for copy in copies:
-        copy.start()
+    copies[0].start()
     total = jnp.sum(stats_ref[...], axis=0)
     mean = total[0:1] * (1.0 / 64)
     gaps = stats_ref[...] - mean[None]
@@ -300,16 +323,24 @@
     mean, gamma, beta = spread[0:1], gain_ref[0:1, :], gain_ref[1:2, :]
     inv = lax.rsqrt(spread[1:2] * (1.0 / CHAN_TOTAL) + 1e-05)
     coef_ref[...] = jnp.concatenate([mean, inv, gamma, beta, jnp.zeros((4, width), f32)], axis=0)
-    coef = jnp.concatenate([mean, inv * gamma, beta, jnp.zeros((5, width), f32)], axis=0).T
+    scaled = [mean, 0.5 * inv * gamma, 0.5 * beta, jnp.zeros((5, width), f32)]
+    coef = jnp.concatenate(scaled, axis=0).T
     for q in range(3):
         wide[q] = jnp.broadcast_to(coef[:, q : q + 1], (width, 128))
 
+    copies[0].wait()
+    for q in [1] + list(range(chunks, len(copies) - 2)) + list(range(2, chunks)):
+        copies[q].start()
+    for copy in copies[-2:]:
+        copy.start()
+
     def activate(j):
-        copies[j].wait()
+        if j > 0:
+            copies[j].wait()
         for at in range(CHUNK * j, CHUNK * j + CHUNK, 128):
             lanes = slice(at, at + 128)
-            normed = (field[:, lanes].astype(f32) - wide[0]) * wide[1] + wide[2]
-            act_ref[:, lanes] = (normed * sigmoid(normed)).astype(bf16)
+            half_normed = (field[:, lanes].astype(f32) - wide[0]) * wide[1] + wide[2]
+            act_ref[:, lanes] = (half_normed + half_normed * jnp.tanh(half_normed)).astype(bf16)
 
     activate(0)
     arrived = chunks
@@ -327,11 +358,11 @@
     pack_taps(0, core_ref[0] == 0, acc, send_ref, keep_ref)
 
 
-def taps_a(core, stats, gain, field_t, before, cot, after):
+def taps_a(core, stats, gain, field_t, before, cot, after, tie):
     width, rows = field_t.shape
     return pl.pallas_call(
         taps_a_kernel,
-        in_specs=[IN_SMEM] + [IN_VMEM] * 2 + [ANYWHERE] * 4,
+        in_specs=[IN_SMEM] + [IN_VMEM] * 2 + [ANYWHERE] * 5,
         out_specs=[IN_VMEM] * 5,
         out_shape=[
             jax.ShapeDtypeStruct((8, width), f32),
@@ -348,7 +379,7 @@
         ],
         compiler_params=params(20),
         cost_estimate=cost(3 * width * rows * width, 10**7, width * rows),
-    )(core, stats, gain, *in_hbm(field_t, before, cot, after))
+    )(core, stats, gain, *in_hbm(field_t, before, cot, after, tie))
 
 
 def taps_b_kernel(core_ref, act_ref, padded_ref, send_ref, keep_ref, acc):
@@ -415,7 +446,7 @@
 
 
 def gradient_kernel(
-    tie_ref, field_ref, prev_ref, cur_ref, next_ref, kernel_ref, coef_ref, held_ref,
+    inner, tie_ref, field_ref, padded_ref, kernel_ref, coef_ref, held_ref,
     out_ref, held_out_ref, sums_ref, sums,
 ):
     step, last = pl.program_id(0), pl.num_programs(0) - 1
@@ -425,18 +456,21 @@
     def _():
         sums[...] = held_ref[...]
 
-    rows_by_rows = (((1,), (1,)), ((), ()))
-    grad = lax.dot_general(next_ref[...], kernel_ref[0], rows_by_rows, preferred_element_type=f32)
-    grad += lax.dot_general(cur_ref[...], kernel_ref[1], rows_by_rows, preferred_element_type=f32)
-    grad += lax.dot_general(prev_ref[...], kernel_ref[2], rows_by_rows, preferred_element_type=f32)
+    frame = 1 + step if inner else 3 * step
+    near = [
+        padded_ref[pl.ds(pl.multiple_of((frame + t) * FRAME, FRAME), FRAME), :]
+        for t in ((1,) if inner else (0, 1, 2))
+    ]
+    cot = near[len(near) // 2].astype(f32)
+    grad = kernel_ref[...] if inner else frame_grad_act(*near, kernel_ref)
     unit = (field_ref[...].astype(f32) - mean) * inv
-    normed = unit * gamma + beta
-    gate = sigmoid(normed)
-    grad = grad * gate * (1.0 + normed * (1.0 - gate))
-    out_ref[...] = grad
+    half_normed = unit * (0.5 * gamma) + 0.5 * beta
+    turn = jnp.tanh(half_normed)
+    grad = grad * (0.5 * ((1.0 + turn) + half_normed * (1.0 - turn * turn)))
+    out_ref[pl.ds(pl.multiple_of(step * FRAME, FRAME), FRAME), :] = cot + (inv * gamma) * grad
     sums[0:1, :] += jnp.sum(grad, axis=0, keepdims=True)
     sums[1:2, :] += jnp.sum(grad * unit, axis=0, keepdims=True)
-    sums[2:3, :] += jnp.sum(cur_ref[...].astype(f32), axis=0, keepdims=True)
+    sums[2:3, :] += jnp.sum(cot, axis=0, keepdims=True)
 
     @pl.when(step == last)
     def _():
@@ -450,28 +484,23 @@
         )
 
 
-def gradient(tie, first, field, padded, kernel, coef, held):
+def gradient(tie, inner, field, padded, kernel, coef, held):
     width = field.shape[1]
-
-    def part(at):
-        return pl.BlockSpec((FRAME, width), lambda i: (first + i + at, 0))
 
     top = pl.BlockSpec((8, width), lambda i: (0, 0))
     return pl.pallas_call(
-        gradient_kernel,
+        functools.partial(gradient_kernel, inner),
         grid=(2,),
         in_specs=[
             ANYWHERE,
-            part(0),
-            part(0),
-            part(1),
-            part(2),
-            pl.BlockSpec(kernel.shape, lambda i: (0, 0, 0)),
+            pl.BlockSpec((FRAME, width), lambda i: (1 + i if inner else 3 * i, 0)),
+            IN_VMEM,
+            pl.BlockSpec((FRAME, width), lambda i: (i, 0)) if inner else IN_VMEM,
             top,
             top,
         ],
         out_specs=[
-            pl.BlockSpec((FRAME, width), lambda i: (i, 0)),
+            IN_VMEM,
             top,
             pl.BlockSpec((16, 128), lambda i: (0, 0)),
         ],
@@ -483,40 +512,40 @@
         scratch_shapes=[pltpu.VMEM((8, width), f32)],
         compiler_params=params(16),
         cost_estimate=cost(1, 1),
-    )(tie, field, padded, padded, padded, kernel, coef, held)
-
-
-def result_kernel(cot_ref, early_ref, late_ref, field_ref, coef_ref, sums_ref, out_ref, means):
+    )(tie, field, padded, kernel, coef, held)
+
+
+def result_kernel(inner_ref, outer_ref, field_ref, coef_ref, sums_ref, out_ref, means):
     @pl.when(pl.program_id(0) == 0)
     def _():
         grouped = jnp.broadcast_to(sums_ref[15:16, :], (8, 128)) * (1.0 / CHAN_TOTAL)
         means[0:1, :] = exact(grouped, group_columns(128, 0))[0:1]
         means[1:2, :] = exact(grouped, group_columns(128, GROUPS))[0:1]
 
-    mean, inv, gamma = (coef_ref[q : q + 1, :] for q in range(3))
+    size, step = out_ref.shape[0], pl.program_id(0)
+    per_frame = FRAME // size
+    inner = (step >= per_frame) & (step < 3 * per_frame)
+    before = jnp.where(inner, per_frame, jnp.where(step < per_frame, 0, 2 * per_frame))
+    rows = pl.ds(pl.multiple_of((step - before) * size, size), size)
+    mean, inv = coef_ref[0:1, :], coef_ref[1:2, :]
     unit = (field_ref[...].astype(f32) - mean) * inv
-    early = 2 * pl.program_id(0) < pl.num_programs(0)
-    for when, grad_ref in ((early, early_ref), (jnp.logical_not(early), late_ref)):
+    taken = inv * (means[0:1, :] + unit * means[1:2, :])
+    for when, grad_ref in ((inner, inner_ref), (jnp.logical_not(inner), outer_ref)):
 
         @pl.when(when)
         def _():
-            out_ref[...] = (
-                cot_ref[...].astype(f32)
-                + inv * (gamma * grad_ref[...] - means[0:1, :] - unit * means[1:2, :])
-            ).astype(bf16)
-
-
-def grad_of_field(cot, early, late, field, coef, sums, block=288):
+            out_ref[...] = (grad_ref[rows, :] - taken).astype(bf16)
+
+
+def grad_of_field(inner, outer, field, coef, sums, block=288):
     rows, width = field.shape
     tile = pl.BlockSpec((block, width), lambda i: (i, 0))
-    half_steps = rows // block // 2
     return pl.pallas_call(
         result_kernel,
         grid=(rows // block,),
         in_specs=[
-            tile,
-            pl.BlockSpec((block, width), lambda i: (jnp.minimum(i, half_steps - 1), 0)),
-            pl.BlockSpec((block, width), lambda i: (jnp.maximum(i - half_steps, 0), 0)),
+            IN_VMEM,
+            IN_VMEM,
             tile,
             pl.BlockSpec((8, width), lambda i: (0, 0)),
             pl.BlockSpec((16, 128), lambda i: (0, 0)),
@@ -526,7 +555,7 @@
         scratch_shapes=[pltpu.VMEM((8, width), f32)],
         compiler_params=params(12),
         cost_estimate=cost(rows * width * 9, rows * width * 10),
-    )(cot, early, late, field, coef, sums)
+    )(inner, outer, field, coef, sums)
 
 
 def per_device(field, cotangent, gamma, beta, kernel):
@@ -546,13 +575,16 @@
     after = lax.ppermute(first, "tm", [(j, i) for i, j in up])
     stats = lax.all_to_all(stats, ("tm", "height"), 0, 0)
     field_t = turned(flat)
-
-    coef, act_t, padded, send_a, keep_a = taps_a(core, stats, gain, field_t, before, cot, after)
+    grad_inner = inner_grad_act(cot, kernel)
+
+    coef, act_t, padded, send_a, keep_a = taps_a(
+        core, stats, gain, field_t, before, cot, after, grad_inner
+    )
     got_a = swap(send_a, "core")
     send_b, keep_b = taps_b(core, act_t, padded)
     got_b = swap(send_b, "core")
     none = jnp.zeros((8, width), f32)
-    grad_early, held, _ = gradient(keep_b, 0, flat, padded, kernel, coef, none)
+    inner, held, _ = gradient(keep_b, True, flat, padded, grad_inner, coef, none)
     kept, got = [keep_a, keep_b], [got_a, got_b]
     sums = [held]
     for step in range(3):
@@ -562,7 +594,7 @@
             lax.ppermute(merged[q][1], AXES, neighbours(NEAR[ORDERS[q][step]])) for q in range(2)
         ]
         if step == 0:
-            grad_late, _, sums = gradient(kept[0], 2, flat, padded, kernel, coef, sums)
+            outer, _, sums = gradient(kept[0], False, flat, padded, kernel, coef, sums)
             sums = [sums]
         elif step == 1:
             sums = [sums, swap(sums, "core"), swap(sums, "z0"), swap(sums, "core", "z0")]
@@ -573,7 +605,7 @@
     taps, sums = far_halve(taps, 2, "z1", own, off, sums)
     taps, sums = far_halve(taps, 1, "x1", own, off, sums)
     taps, sums = far_halve(taps, 0, "z2", own, off, sums)
-    field_grad = grad_of_field(cot, grad_early, grad_late, flat, coef, sums)
+    field_grad = grad_of_field(inner, outer, flat, coef, sums)
 
     got, sums = far_swap(taps, sums, "yh")
     taps = taps + got

time: 118 us -> 115 us (0.975)
  waiting for transfers between devices: 30.6 us -> 19.1 us
  Pallas kernels: 42.9 us -> 48.2 us
  starting transfers between devices: 40.6 us -> 44.7 us
    all_to_all x1, waiting for transfers between devices: 7.48 us -> 0.01 us  [per_device(): stats = lax.all_to_all(stats, ('tm', 'height'), 0, 0)]
    pallas_call x3 -> x4, Pallas kernels: 18.3 us -> 23.3 us  [the longest x2 9.97 us: gradient(): pl.pallas_call(functools.partial(gradient_kernel, inner), grid=(2,), in_s...]
    ppermute x12, starting transfers between devices: 12.6 us -> 17.1 us  [swap(): return lax.ppermute(value, AXES, chosen)]
    ppermute x12, waiting for transfers between devices: 20.4 us -> 16.2 us  [swap(): return lax.ppermute(value, AXES, chosen)]
  transfers between devices with their start and end apart: 21 -> 21, of which waited for: 9 -> 7; matrix products, arithmetic and copies ran while one was open for 0% -> 0% of each run, Pallas kernels for 19% -> 23%
where the time goes in v1:
time: 115 us
  Pallas kernels  48.2 us (42%)
  starting transfers between devices  44.7 us (39%)
  waiting for transfers between devices  19.1 us (17%)
    ppermute x12, starting transfers between devices, swap(): return lax.ppermute(value, AXES, chosen)  17.1 us
    ppermute x12, waiting for transfers between devices, swap(): return lax.ppermute(value, AXES, chosen)  16.2 us
    all_to_all x1, starting transfers between devices, per_device(): stats = lax.all_to_all(stats, ('tm', 'height'), 0, 0)  10.4 us
    pallas_call x2, Pallas kernels, gradient(): pl.pallas_call(functools.partial(gradient_kernel, inner), grid=(2,), in_s...  9.97 us
    pallas_call x1, Pallas kernels, taps_a(): pl.pallas_call(taps_a_kernel, in_specs=[IN_SMEM] + [IN_VMEM] * 2 + [ANYWH...  8.91 us
    pallas_call x1, Pallas kernels, inner_grad_act(): pl.pallas_call(grad_act_kernel, grid=(2,), in_specs=[part(0), part(1), pa...  8.02 us
    ppermute x6, starting transfers between devices, per_device(): lax.ppermute(merged[q][1], AXES, neighbours(NEAR[ORDERS[q][step]]))  7.46 us
    pallas_call x1, Pallas kernels, local_stats(): pl.pallas_call(stats_kernel, grid=(BLOCKS // 2,), in_specs=[IN_SMEM, pl.B...  6.37 us
  transfers between devices with their start and end apart: 21, of which 7 were waited for; matrix products, arithmetic and copies ran while one was open for 0% of the time, Pallas kernels for 23%

profile of v1, /device:TPU:2, one launch (start us, length us, event | category | flops | bytes accessed | tf_op | source)
XLA Modules:
  0.0 115.0 jit_solution(8901311448209510018)
XLA Ops:
  0.8 6.4 %shard_map.76 = (f32[64,2,128]{2,1,0:T(2,128)}, bf16[576,640]{1,0:T(8,128)(2,1)}, bf16[576,640]{1,0:T(8,128)(2,1)}) custom-call(s32[16]{0:T(128)S(1)} %stack.73.bits_ref, bf16[2304,640]{1,0:T(8,128)(2,1)} %bitcast.55, bf16[2304,640]{1,0:T(8,128)(2,1)} %bitcast.56, bf16[2304,640]{1,0:T(8,128)(2,1)} %bitcast.61, bf16[2304,640]{1,0:T(8,128)(2,1)} %bitcast.62), custom_call_target="tpu_custom_call" | custom-call | flops 5898240 | bytes 2949120 | tf_op jit(solution)/shard_map/pallas_call | solution.py:153
  7.2 3.8 %collective-permute-start = (bf16[576,640]{1,0:T(8,128)(2,1)}, bf16[576,640]{1,0:T(8,128)(2,1)}, u32[]{:S(2)}, u32[]{:S(2)}) collective-permute-start(bf16[576,640]{1,0:T(8,128)(2,1)} %get-tuple-element.33), channel_id=1, source_target_pairs={{0,2},{2,4},{4,6},{6,8},{8,10},{10,12},{12,14},{14,16},{16,18},{18... | collective-permute-start | bytes 2211848 | tf_op jit(solution)/shard_map/ppermute | solution.py:574
  11.0 5.8 %collective-permute-start.1 = (bf16[576,640]{1,0:T(8,128)(2,1)}, bf16[576,640]{1,0:T(8,128)(2,1)}, u32[]{:S(2)}, u32[]{:S(2)}) collective-permute-start(bf16[576,640]{1,0:T(8,128)(2,1)} %get-tuple-element.34), channel_id=1, source_target_pairs={{2,0},{4,2},{6,4},{8,6},{10,8},{12,10},{14,12},{16,14},{18,16},{20... | collective-permute-start | bytes 2211848 | tf_op jit(solution)/shard_map/ppermute | solution.py:575
  16.8 10.4 %all-to-all-start = ((f32[64,2,128]{2,1,0:T(2,128)}), f32[64,2,128]{2,1,0:T(2,128)S(1)}, u32[]{:S(2)}, u32[]{:S(2)}) async-start(f32[64,2,128]{2,1,0:T(2,128)} %get-tuple-element.32), calls=%async_computation | async-start | bytes 131072 | tf_op jit(solution)/shard_map/all_to_all | solution.py:576
  27.5 3.4 %shard_map.77.field_ref = bf16[640,2304]{1,0:T(8,128)(2,1)} custom-call(bf16[2304,640]{1,0:T(8,128)(2,1)S(1)} %bitcast.57), custom_call_target="tpu_custom_call" | custom-call | flops 1000000000 | bytes 10000000 | tf_op jit(solution)/shard_map/pallas_call | solution.py:188
  30.9 8.0 %shard_map.78.tie_ref.kernel_ref = f32[1152,640]{1,0:T(8,128)} custom-call(bf16[2304,640]{1,0:T(8,128)(2,1)} %bitcast.63, bf16[2304,640]{1,0:T(8,128)(2,1)} %bitcast.64, bf16[2304,640]{1,0:T(8,128)(2,1)} %bitcast.65, bf16[3,640,640]{2,1,0:T(8,128)(2,1)} %kernel_ref.3), custom_call_target="tpu_custom_call" | custom-call | flops 1000000000 | bytes 10000000 | tf_op jit(solution)/shard_map/pallas_call | solution.py:216
  38.9 8.9 %shard_map.79 = (f32[8,640]{1,0:T(8,128)S(1)}, bf16[640,2304]{1,0:T(8,128)(2,1)S(1)}, bf16[3456,640]{1,0:T(8,128)(2,1)S(1)}, bf16[32,80,128]{2,1,0:T(8,128)(2,1)S(1)}, f32[32,80,128]{2,1,0:T(8,128)S(1)}) custom-call(s32[1]{0:T(128)} %bitcast.core_ref, f32[64,2,128]{2,1,0:T(2,128)S(1)} %all-to-all-done.stats_ref, f32[8,640]{1,0:T(8,128)S(1)} %maximum_maximum_fusion.gain_ref, ...), custom_call_target="tpu_custom_call" | custom-call | flops 2831155200 | bytes 10000000 | tf_op jit(solution)/shard_map/pallas_call | solution.py:363
  47.8 4.1 %shard_map.80 = (bf16[32,80,128]{2,1,0:T(8,128)(2,1)S(1)}, f32[32,80,128]{2,1,0:T(8,128)S(1)}) custom-call(s32[1]{0:T(128)} %bitcast.core_ref, bf16[640,2304]{1,0:T(8,128)(2,1)S(1)} %get-tuple-element.35.act_ref, bf16[3456,640]{1,0:T(8,128)(2,1)S(1)} %get-tuple-element.36.padded_ref), custom_call_target="tpu_custom_call" | custom-call | flops 2831155200 | bytes 10000000 | tf_op jit(solution)/shard_map/pallas_call | solution.py:395
  52.6 3.3 %shard_map.81 = (f32[1152,640]{1,0:T(8,128)S(1)}, f32[8,640]{1,0:T(8,128)S(1)}, f32[16,128]{1,0:T(8,128)}) custom-call(f32[32,80,128]{2,1,0:T(8,128)S(1)} %get-tuple-element.37.tie_ref.refs_2_, bf16[2304,640]{1,0:T(8,128)(2,1)S(1)} %bitcast.58, bf16[3456,640]{1,0:T(8,128)(2,1)S(1)} %get-tuple-element.36.padded_ref, f32[1152,640]{1,0:T(8,128)S(1)} %copy-done.1, ...), custom_call_target="tpu_custom_call" | custom-call | flops 1 | bytes 1 | tf_op jit(solution)/shard_map/pallas_call | solution.py:491
  56.7 3.1 %collective-permute-start.4 = (bf16[16,80,128]{2,1,0:T(8,128)(2,1)S(1)}, bf16[16,80,128]{2,1,0:T(8,128)(2,1)S(1)}, u32[]{:S(2)}, u32[]{:S(2)}) collective-permute-start(bf16[16,80,128]{2,1,0:T(8,128)(2,1)S(1)} %get-tuple-element.47), channel_id=1, source_target_pairs={{0,2},{1,3},{2,0},{3,1},{4,6},{5,7},{6,4},{7,5},{8,10},{9,11},{10,... | collective-permute-start | bytes 983048 | tf_op jit(solution)/shard_map/ppermute | solution.py:594
  60.4 6.7 %shard_map.83 = (f32[1152,640]{1,0:T(8,128)S(1)}, f32[8,640]{1,0:T(8,128)}, f32[16,128]{1,0:T(8,128)S(1)}) custom-call(f32[16,80,128]{2,1,0:T(8,128)S(1)} %get-tuple-element.44.tie_ref.refs_0_, bf16[2304,640]{1,0:T(8,128)(2,1)S(1)} %bitcast.59, bf16[3456,640]{1,0:T(8,128)(2,1)S(1)} %get-tuple-element.36.padded_ref, bf16[3,640,640]{2,1,0:T(8,128)(2,1)S(1)} %copy-done.2, ...), custom_call_target="tpu_custom_call" | custom-call | flops 1 | bytes 1 | tf_op jit(solution)/shard_map/pallas_call | solution.py:491
  67.7 1.5 %collective-permute-start.6 = (bf16[8,80,128]{2,1,0:T(8,128)(2,1)S(1)}, bf16[8,80,128]{2,1,0:T(8,128)(2,1)S(1)}, u32[]{:S(2)}, u32[]{:S(2)}) collective-permute-start(bf16[8,80,128]{2,1,0:T(8,128)(2,1)S(1)} %get-tuple-element.52), channel_id=1, source_target_pairs={{0,16},{1,17},{2,18},{3,19},{4,20},{5,21},{6,22},{7,23},{8,24},{9,... | collective-permute-start | bytes 491528 | tf_op jit(solution)/shard_map/ppermute | solution.py:594
  69.4 1.6 %collective-permute-start.10 = (f32[16,128]{1,0:T(8,128)S(1)}, f32[16,128]{1,0:T(8,128)S(1)}, u32[]{:S(2)}, u32[]{:S(2)}) collective-permute-start(f32[16,128]{1,0:T(8,128)S(1)} %get-tuple-element.55.refs_4_), channel_id=1, source_target_pairs={{0,66},{1,67},{2,64},{3,65},{4,70},{5,71},{6,68},{7,69},{8,74},{9,... | collective-permute-start | bytes 24584 | tf_op jit(solution)/shard_map/ppermute | solution.py:72
  72.8 2.3 %collective-permute-done.9.refs_6_ = f32[16,128]{1,0:T(8,128)S(1)} collective-permute-done((f32[16,128]{1,0:T(8,128)S(1)}, f32[16,128]{1,0:T(8,128)S(1)}, u32[]{:S(2)}, u32[]{:S(2)}) %collective-permute-start.9) | collective-permute-done | bytes 8224 | tf_op jit(solution)/shard_map/ppermute | solution.py:72
  75.7 1.7 %collective-permute-start.11 = (f32[16,128]{1,0:T(8,128)S(1)}, f32[16,128]{1,0:T(8,128)S(1)}, u32[]{:S(2)}, u32[]{:S(2)}) collective-permute-start(f32[16,128]{1,0:T(8,128)S(1)} %get-tuple-element.56), channel_id=1, source_target_pairs={{0,16},{1,17},{2,18},{3,19},{4,20},{5,21},{6,22},{7,23},{8,24},{9,... | collective-permute-start | bytes 24584 | tf_op jit(solution)/shard_map/ppermute | solution.py:72
  79.2 1.7 %collective-permute-start.15 = (bf16[4,80,128]{2,1,0:T(8,128)(2,1)S(1)}, bf16[4,80,128]{2,1,0:T(8,128)(2,1)S(1)}, u32[]{:S(2)}, u32[]{:S(2)}) collective-permute-start(bf16[4,80,128]{2,1,0:T(8,128)(2,1)S(1)} %get-tuple-element.60), channel_id=1, source_target_pairs={{0,16},{1,17},{2,18},{3,19},{4,20},{5,21},{6,22},{7,23},{8,24},{9,... | collective-permute-start | bytes 245768 | tf_op jit(solution)/shard_map/ppermute | solution.py:594
  83.7 1.6 %collective-permute-done.14 = bf16[4,80,128]{2,1,0:T(8,128)(2,1)S(1)} collective-permute-done((bf16[4,80,128]{2,1,0:T(8,128)(2,1)S(1)}, bf16[4,80,128]{2,1,0:T(8,128)(2,1)S(1)}, u32[]{:S(2)}, u32[]{:S(2)}) %collective-permute-start.14) | collective-permute-done | bytes 81952 | tf_op jit(solution)/shard_map/ppermute | solution.py:594
  85.4 3.8 %collective-permute-start.16 = (bf16[368,128]{1,0:T(8,128)(2,1)S(1)}, bf16[368,128]{1,0:T(8,128)(2,1)S(1)}, u32[]{:S(2)}, u32[]{:S(2)}) collective-permute-start(bf16[368,128]{1,0:T(8,128)(2,1)S(1)} %pad_maximum_fusion), channel_id=1, source_target_pairs={{0,4},{1,5},{2,6},{3,7},{4,0},{5,1},{6,2},{7,3},{8,12},{9,13},{10,... | collective-permute-start | bytes 282632 | tf_op jit(solution)/shard_map/ppermute | solution.py:72
  89.2 3.6 %collective-permute-done.16 = bf16[368,128]{1,0:T(8,128)(2,1)S(1)} collective-permute-done((bf16[368,128]{1,0:T(8,128)(2,1)S(1)}, bf16[368,128]{1,0:T(8,128)(2,1)S(1)}, u32[]{:S(2)}, u32[]{:S(2)}) %collective-permute-start.16) | collective-permute-done | bytes 94240 | tf_op jit(solution)/shard_map/ppermute | solution.py:72
  93.3 5.3 %collective-permute-done.17 = bf16[208,128]{1,0:T(8,128)(2,1)S(1)} collective-permute-done((bf16[208,128]{1,0:T(8,128)(2,1)S(1)}, bf16[208,128]{1,0:T(8,128)(2,1)S(1)}, u32[]{:S(2)}, u32[]{:S(2)}) %collective-permute-start.17) | collective-permute-done | bytes 53280 | tf_op jit(solution)/shard_map/ppermute | solution.py:72
  98.8 3.9 %collective-permute-start.18 = (bf16[128,128]{1,0:T(8,128)(2,1)S(1)}, bf16[128,128]{1,0:T(8,128)(2,1)S(1)}, u32[]{:S(2)}, u32[]{:S(2)}) collective-permute-start(bf16[128,128]{1,0:T(8,128)(2,1)S(1)} %pad_maximum_fusion.4), channel_id=1, source_target_pairs={{0,8},{1,9},{2,10},{3,11},{4,12},{5,13},{6,14},{7,15},{8,0},{9,1},... | collective-permute-start | bytes 98312 | tf_op jit(solution)/shard_map/ppermute | solution.py:72
  102.7 4.0 %collective-permute-done.18 = bf16[128,128]{1,0:T(8,128)(2,1)S(1)} collective-permute-done((bf16[128,128]{1,0:T(8,128)(2,1)S(1)}, bf16[128,128]{1,0:T(8,128)(2,1)S(1)}, u32[]{:S(2)}, u32[]{:S(2)}) %collective-permute-start.18) | collective-permute-done | bytes 32800 | tf_op jit(solution)/shard_map/ppermute | solution.py:72
  106.7 1.5 %collective-permute-start.19 = (bf16[128,128]{1,0:T(8,128)(2,1)S(1)}, bf16[128,128]{1,0:T(8,128)(2,1)S(1)}, u32[]{:S(2)}, u32[]{:S(2)}) collective-permute-start(bf16[128,128]{1,0:T(8,128)(2,1)S(1)} %pad_maximum_fusion.5), channel_id=1, source_target_pairs={{0,128},{1,129},{2,130},{3,131},{4,132},{5,133},{6,134},{7,135},{8... | collective-permute-start | bytes 98312 | tf_op jit(solution)/shard_map/ppermute | solution.py:72
  108.2 5.3 %shard_map.86 = bf16[2304,640]{1,0:T(8,128)(2,1)} custom-call(f32[1152,640]{1,0:T(8,128)S(1)} %get-tuple-element.39.inner_ref, f32[1152,640]{1,0:T(8,128)S(1)} %get-tuple-element.46.outer_ref, bf16[2304,640]{1,0:T(8,128)(2,1)S(1)} %bitcast.60, f32[8,640]{1,0:T(8,128)S(1)} %get-tuple-element.38.coef_ref, f32[16,128]{1,0:T(8,128)S(1)} %get-tuple-element.62.sums_ref), custom_call_target="tpu_custom_call" | custom-call | flops 13271040 | bytes 14745600 | tf_op jit(solution)/shard_map/pallas_call | solution.py:543
  (84 shorter events, 12.2 us)
Async XLA Ops:
  0.7 26.5 %copy-start.3 = (f32[640]{0:T(1024)S(1)}, f32[640]{0:T(1024)}, u32[]{:S(2)}) copy-start(f32[640]{0:T(1024)} %param.7) | copy-start | bytes 7684
  0.8 26.5 %copy-start.4 = (f32[640]{0:T(1024)S(1)}, f32[640]{0:T(1024)}, u32[]{:S(2)}) copy-start(f32[640]{0:T(1024)} %param.8) | copy-start | bytes 7684
  0.8 26.7 %copy-start = (bf16[1,4,9,64,640]{4,3,2,1,0:T(8,128)(2,1)S(1)}, bf16[1,4,9,64,640]{4,3,2,1,0:T(8,128)(2,1)}, u32[]{:S(2)}) copy-start(bf16[1,4,9,64,640]{4,3,2,1,0:T(8,128)(2,1)} %param.5) | copy-start | bytes 8847364
  7.2 31.7 %collective-permute-start = (bf16[576,640]{1,0:T(8,128)(2,1)}, bf16[576,640]{1,0:T(8,128)(2,1)}, u32[]{:S(2)}, u32[]{:S(2)}) collective-permute-start(bf16[576,640]{1,0:T(8,128)(2,1)} %get-tuple-element.33), channel_id=1, source_target_pairs={{0,2},{2,4},{4,6},{6,8},{8,10},{10,12},{12,14},{14,16},{16,18},{18... | collective-permute-start | bytes 2211848 | tf_op jit(solution)/shard_map/ppermute | solution.py:574
  11.0 27.9 %collective-permute-start.1 = (bf16[576,640]{1,0:T(8,128)(2,1)}, bf16[576,640]{1,0:T(8,128)(2,1)}, u32[]{:S(2)}, u32[]{:S(2)}) collective-permute-start(bf16[576,640]{1,0:T(8,128)(2,1)} %get-tuple-element.34), channel_id=1, source_target_pairs={{2,0},{4,2},{6,4},{8,6},{10,8},{12,10},{14,12},{16,14},{18,16},{20... | collective-permute-start | bytes 2211848 | tf_op jit(solution)/shard_map/ppermute | solution.py:575
  16.8 22.1 %all-to-all-start = ((f32[64,2,128]{2,1,0:T(2,128)}), f32[64,2,128]{2,1,0:T(2,128)S(1)}, u32[]{:S(2)}, u32[]{:S(2)}) async-start(f32[64,2,128]{2,1,0:T(2,128)} %get-tuple-element.32), calls=%async_computation | async-start | bytes 131072 | tf_op jit(solution)/shard_map/all_to_all | solution.py:576
  52.0 3.9 %collective-permute-start.3 = (bf16[32,80,128]{2,1,0:T(8,128)(2,1)S(1)}, bf16[32,80,128]{2,1,0:T(8,128)(2,1)S(1)}, u32[]{:S(2)}, u32[]{:S(2)}) collective-permute-start(bf16[32,80,128]{2,1,0:T(8,128)(2,1)S(1)} %get-tuple-element.42), channel_id=1, source_target_pairs={{0,64},{1,65},{2,66},{3,67},{4,68},{5,69},{6,70},{7,71},{8,72},{9,... | collective-permute-start | bytes 1966088 | tf_op jit(solution)/shard_map/ppermute | solution.py:72
  52.1 3.8 %collective-permute-start.2 = (bf16[32,80,128]{2,1,0:T(8,128)(2,1)S(1)}, bf16[32,80,128]{2,1,0:T(8,128)(2,1)S(1)}, u32[]{:S(2)}, u32[]{:S(2)}) collective-permute-start(bf16[32,80,128]{2,1,0:T(8,128)(2,1)S(1)} %get-tuple-element.41), channel_id=1, source_target_pairs={{0,64},{1,65},{2,66},{3,67},{4,68},{5,69},{6,70},{7,71},{8,72},{9,... | collective-permute-start | bytes 1966088 | tf_op jit(solution)/shard_map/ppermute | solution.py:72
  56.7 10.3 %collective-permute-start.4 = (bf16[16,80,128]{2,1,0:T(8,128)(2,1)S(1)}, bf16[16,80,128]{2,1,0:T(8,128)(2,1)S(1)}, u32[]{:S(2)}, u32[]{:S(2)}) collective-permute-start(bf16[16,80,128]{2,1,0:T(8,128)(2,1)S(1)} %get-tuple-element.47), channel_id=1, source_target_pairs={{0,2},{1,3},{2,0},{3,1},{4,6},{5,7},{6,4},{7,5},{8,10},{9,11},{10,... | collective-permute-start | bytes 983048 | tf_op jit(solution)/shard_map/ppermute | solution.py:594
  59.8 7.3 %collective-permute-start.5 = (bf16[16,80,128]{2,1,0:T(8,128)(2,1)S(1)}, bf16[16,80,128]{2,1,0:T(8,128)(2,1)S(1)}, u32[]{:S(2)}, u32[]{:S(2)}) collective-permute-start(bf16[16,80,128]{2,1,0:T(8,128)(2,1)S(1)} %get-tuple-element.49), channel_id=1, source_target_pairs={{0,1},{1,0},{2,3},{3,2},{4,5},{5,4},{6,7},{7,6},{8,9},{9,8},{10,11... | collective-permute-start | bytes 983048 | tf_op jit(solution)/shard_map/ppermute | solution.py:594
  67.7 7.3 %collective-permute-start.6 = (bf16[8,80,128]{2,1,0:T(8,128)(2,1)S(1)}, bf16[8,80,128]{2,1,0:T(8,128)(2,1)S(1)}, u32[]{:S(2)}, u32[]{:S(2)}) collective-permute-start(bf16[8,80,128]{2,1,0:T(8,128)(2,1)S(1)} %get-tuple-element.52), channel_id=1, source_target_pairs={{0,16},{1,17},{2,18},{3,19},{4,20},{5,21},{6,22},{7,23},{8,24},{9,... | collective-permute-start | bytes 491528 | tf_op jit(solution)/shard_map/ppermute | solution.py:594
  69.2 5.8 %collective-permute-start.7 = (bf16[8,80,128]{2,1,0:T(8,128)(2,1)S(1)}, bf16[8,80,128]{2,1,0:T(8,128)(2,1)S(1)}, u32[]{:S(2)}, u32[]{:S(2)}) collective-permute-start(bf16[8,80,128]{2,1,0:T(8,128)(2,1)S(1)} %get-tuple-element.54), channel_id=1, source_target_pairs={{0,2},{1,3},{2,0},{3,1},{4,6},{5,7},{6,4},{7,5},{8,10},{9,11},{10,... | collective-permute-start | bytes 491528 | tf_op jit(solution)/shard_map/ppermute | solution.py:594
  69.4 3.3 %collective-permute-start.10 = (f32[16,128]{1,0:T(8,128)S(1)}, f32[16,128]{1,0:T(8,128)S(1)}, u32[]{:S(2)}, u32[]{:S(2)}) collective-permute-start(f32[16,128]{1,0:T(8,128)S(1)} %get-tuple-element.55.refs_4_), channel_id=1, source_target_pairs={{0,66},{1,67},{2,64},{3,65},{4,70},{5,71},{6,68},{7,69},{8,74},{9,... | collective-permute-start | bytes 24584 | tf_op jit(solution)/shard_map/ppermute | solution.py:72
  71.0 1.8 %collective-permute-start.8 = (f32[16,128]{1,0:T(8,128)S(1)}, f32[16,128]{1,0:T(8,128)S(1)}, u32[]{:S(2)}, u32[]{:S(2)}) collective-permute-start(f32[16,128]{1,0:T(8,128)S(1)} %get-tuple-element.55.refs_4_), channel_id=1, source_target_pairs={{0,64},{1,65},{2,66},{3,67},{4,68},{5,69},{6,70},{7,71},{8,72},{9,... | collective-permute-start | bytes 24584 | tf_op jit(solution)/shard_map/ppermute | solution.py:72
  71.4 3.7 %collective-permute-start.9 = (f32[16,128]{1,0:T(8,128)S(1)}, f32[16,128]{1,0:T(8,128)S(1)}, u32[]{:S(2)}, u32[]{:S(2)}) collective-permute-start(f32[16,128]{1,0:T(8,128)S(1)} %get-tuple-element.55.refs_4_), channel_id=1, source_target_pairs={{0,2},{1,3},{2,0},{3,1},{4,6},{5,7},{6,4},{7,5},{8,10},{9,11},{10,... | collective-permute-start | bytes 24584 | tf_op jit(solution)/shard_map/ppermute | solution.py:72
  75.7 5.7 %collective-permute-start.11 = (f32[16,128]{1,0:T(8,128)S(1)}, f32[16,128]{1,0:T(8,128)S(1)}, u32[]{:S(2)}, u32[]{:S(2)}) collective-permute-start(f32[16,128]{1,0:T(8,128)S(1)} %get-tuple-element.56), channel_id=1, source_target_pairs={{0,16},{1,17},{2,18},{3,19},{4,20},{5,21},{6,22},{7,23},{8,24},{9,... | collective-permute-start | bytes 24584 | tf_op jit(solution)/shard_map/ppermute | solution.py:72
  77.4 3.9 %collective-permute-start.12 = (f32[16,128]{1,0:T(8,128)S(1)}, f32[16,128]{1,0:T(8,128)S(1)}, u32[]{:S(2)}, u32[]{:S(2)}) collective-permute-start(f32[16,128]{1,0:T(8,128)S(1)} %get-tuple-element.56), channel_id=1, source_target_pairs={{0,1},{1,0},{2,3},{3,2},{4,5},{5,4},{6,7},{7,6},{8,9},{9,8},{10,11... | collective-permute-start | bytes 24584 | tf_op jit(solution)/shard_map/ppermute | solution.py:72
  77.9 4.5 %collective-permute-start.13 = (f32[16,128]{1,0:T(8,128)S(1)}, f32[16,128]{1,0:T(8,128)S(1)}, u32[]{:S(2)}, u32[]{:S(2)}) collective-permute-start(f32[16,128]{1,0:T(8,128)S(1)} %get-tuple-element.56), channel_id=1, source_target_pairs={{0,17},{1,16},{2,19},{3,18},{4,21},{5,20},{6,23},{7,22},{8,25},{9,... | collective-permute-start | bytes 24584 | tf_op jit(solution)/shard_map/ppermute | solution.py:72
  79.2 4.4 %collective-permute-start.15 = (bf16[4,80,128]{2,1,0:T(8,128)(2,1)S(1)}, bf16[4,80,128]{2,1,0:T(8,128)(2,1)S(1)}, u32[]{:S(2)}, u32[]{:S(2)}) collective-permute-start(bf16[4,80,128]{2,1,0:T(8,128)(2,1)S(1)} %get-tuple-element.60), channel_id=1, source_target_pairs={{0,16},{1,17},{2,18},{3,19},{4,20},{5,21},{6,22},{7,23},{8,24},{9,... | collective-permute-start | bytes 245768 | tf_op jit(solution)/shard_map/ppermute | solution.py:594
  80.9 4.4 %collective-permute-start.14 = (bf16[4,80,128]{2,1,0:T(8,128)(2,1)S(1)}, bf16[4,80,128]{2,1,0:T(8,128)(2,1)S(1)}, u32[]{:S(2)}, u32[]{:S(2)}) collective-permute-start(bf16[4,80,128]{2,1,0:T(8,128)(2,1)S(1)} %get-tuple-element.58), channel_id=1, source_target_pairs={{0,1},{1,0},{2,3},{3,2},{4,5},{5,4},{6,7},{7,6},{8,9},{9,8},{10,11... | collective-permute-start | bytes 245768 | tf_op jit(solution)/shard_map/ppermute | solution.py:594
  85.4 7.4 %collective-permute-start.16 = (bf16[368,128]{1,0:T(8,128)(2,1)S(1)}, bf16[368,128]{1,0:T(8,128)(2,1)S(1)}, u32[]{:S(2)}, u32[]{:S(2)}) collective-permute-start(bf16[368,128]{1,0:T(8,128)(2,1)S(1)} %pad_maximum_fusion), channel_id=1, source_target_pairs={{0,4},{1,5},{2,6},{3,7},{4,0},{5,1},{6,2},{7,3},{8,12},{9,13},{10,... | collective-permute-start | bytes 282632 | tf_op jit(solution)/shard_map/ppermute | solution.py:72
  92.9 5.7 %collective-permute-start.17 = (bf16[208,128]{1,0:T(8,128)(2,1)S(1)}, bf16[208,128]{1,0:T(8,128)(2,1)S(1)}, u32[]{:S(2)}, u32[]{:S(2)}) collective-permute-start(bf16[208,128]{1,0:T(8,128)(2,1)S(1)} %pad_maximum_fusion.1), channel_id=1, source_target_pairs={{0,32},{1,33},{2,34},{3,35},{4,36},{5,37},{6,38},{7,39},{8,40},{9,... | collective-permute-start | bytes 159752 | tf_op jit(solution)/shard_map/ppermute | solution.py:72
  98.8 7.9 %collective-permute-start.18 = (bf16[128,128]{1,0:T(8,128)(2,1)S(1)}, bf16[128,128]{1,0:T(8,128)(2,1)S(1)}, u32[]{:S(2)}, u32[]{:S(2)}) collective-permute-start(bf16[128,128]{1,0:T(8,128)(2,1)S(1)} %pad_maximum_fusion.4), channel_id=1, source_target_pairs={{0,8},{1,9},{2,10},{3,11},{4,12},{5,13},{6,14},{7,15},{8,0},{9,1},... | collective-permute-start | bytes 98312 | tf_op jit(solution)/shard_map/ppermute | solution.py:72
  106.7 6.7 %collective-permute-start.19 = (bf16[128,128]{1,0:T(8,128)(2,1)S(1)}, bf16[128,128]{1,0:T(8,128)(2,1)S(1)}, u32[]{:S(2)}, u32[]{:S(2)}) collective-permute-start(bf16[128,128]{1,0:T(8,128)(2,1)S(1)} %pad_maximum_fusion.5), channel_id=1, source_target_pairs={{0,128},{1,129},{2,130},{3,131},{4,132},{5,133},{6,134},{7,135},{8... | collective-permute-start | bytes 98312 | tf_op jit(solution)/shard_map/ppermute | solution.py:72
  (2 other events, 9.2 us)

commit v2 on v1

--- a/solution.py
+++ b/solution.py
@@ -335,7 +335,7 @@
         copy.start()
 
     def activate(j):
-        if j > 0:
+        if j == 1:
             copies[j].wait()
         for at in range(CHUNK * j, CHUNK * j + CHUNK, 128):
             lanes = slice(at, at + 128)
@@ -343,17 +343,17 @@
             act_ref[:, lanes] = (half_normed + half_normed * jnp.tanh(half_normed)).astype(bf16)
 
     activate(0)
-    arrived = chunks
-    for j in range(chunks):
+    activate(1)
+    needed = chunks + (2 * FRAME + CHUNK - 1) // FRAME + 1
+    for copy in copies[chunks:needed]:
+        copy.wait()
+    add_taps(0, acc, act_ref, padded_ref, 0)
+    for copy in copies[needed:] + copies[2:chunks]:
+        copy.wait()
+    for j in range(1, chunks):
         if j + 1 < chunks:
             activate(j + 1)
-        needed = chunks + (2 * FRAME + CHUNK * (j + 1) - 1) // FRAME + 1
-        for copy in copies[arrived:needed]:
-            copy.wait()
-        arrived = needed
         add_taps(0, acc, act_ref, padded_ref, j)
-    for copy in copies[arrived:]:
-        copy.wait()
     acc[960:, :] = jnp.zeros((8, width), f32)
     pack_taps(0, core_ref[0] == 0, acc, send_ref, keep_ref)
 
@@ -445,9 +445,12 @@
     return [(out[2 * q], out[2 * q + 1]) for q in range(len(chains))], out[-1]
 
 
+PART = FRAME
+
+
 def gradient_kernel(
     inner, tie_ref, field_ref, padded_ref, kernel_ref, coef_ref, held_ref,
-    out_ref, held_out_ref, sums_ref, sums,
+    out_ref, field_out_ref, held_out_ref, sums_ref, sums,
 ):
     step, last = pl.program_id(0), pl.num_programs(0) - 1
     mean, inv, gamma, beta = (coef_ref[q : q + 1, :] for q in range(4))
@@ -457,20 +460,24 @@
         sums[...] = held_ref[...]
 
     frame = 1 + step if inner else 3 * step
-    near = [
-        padded_ref[pl.ds(pl.multiple_of((frame + t) * FRAME, FRAME), FRAME), :]
-        for t in ((1,) if inner else (0, 1, 2))
-    ]
-    cot = near[len(near) // 2].astype(f32)
-    grad = kernel_ref[...] if inner else frame_grad_act(*near, kernel_ref)
-    unit = (field_ref[...].astype(f32) - mean) * inv
-    half_normed = unit * (0.5 * gamma) + 0.5 * beta
-    turn = jnp.tanh(half_normed)
-    grad = grad * (0.5 * ((1.0 + turn) + half_normed * (1.0 - turn * turn)))
-    out_ref[pl.ds(pl.multiple_of(step * FRAME, FRAME), FRAME), :] = cot + (inv * gamma) * grad
-    sums[0:1, :] += jnp.sum(grad, axis=0, keepdims=True)
-    sums[1:2, :] += jnp.sum(grad * unit, axis=0, keepdims=True)
-    sums[2:3, :] += jnp.sum(cot, axis=0, keepdims=True)
+    for part in range(0, FRAME, PART):
+        near = [
+            padded_ref[pl.ds(pl.multiple_of((frame + t) * FRAME + part, 16), PART), :]
+            for t in ((1,) if inner else (0, 1, 2))
+        ]
+        cot = near[len(near) // 2].astype(f32)
+        grad = kernel_ref[part : part + PART, :] if inner else frame_grad_act(*near, kernel_ref)
+        field = field_ref[part : part + PART, :]
+        unit = (field.astype(f32) - mean) * inv
+        half_normed = unit * (0.5 * gamma) + 0.5 * beta
+        turn = jnp.tanh(half_normed)
+        grad = grad * (0.5 * ((1.0 + turn) + half_normed * (1.0 - turn * turn)))
+        rows = pl.ds(pl.multiple_of(step * FRAME + part, 16), PART)
+        out_ref[rows, :] = cot + (inv * gamma) * grad
+        field_out_ref[rows, :] = field
+        sums[0:1, :] += jnp.sum(grad, axis=0, keepdims=True)
+        sums[1:2, :] += jnp.sum(grad * unit, axis=0, keepdims=True)
+        sums[2:3, :] += jnp.sum(cot, axis=0, keepdims=True)
 
     @pl.when(step == last)
     def _():
@@ -501,11 +508,13 @@
         ],
         out_specs=[
             IN_VMEM,
+            IN_VMEM,
             top,
             pl.BlockSpec((16, 128), lambda i: (0, 0)),
         ],
         out_shape=[
             vmem((2 * FRAME, width), f32),
+            vmem((2 * FRAME, width), bf16),
             jax.ShapeDtypeStruct((8, width), f32),
             jax.ShapeDtypeStruct((16, 128), f32),
         ],
@@ -515,7 +524,7 @@
     )(tie, field, padded, kernel, coef, held)
 
 
-def result_kernel(inner_ref, outer_ref, field_ref, coef_ref, sums_ref, out_ref, means):
+def result_kernel(inner_ref, outer_ref, inner_field_ref, outer_field_ref, coef_ref, sums_ref, out_ref, means):
     @pl.when(pl.program_id(0) == 0)
     def _():
         grouped = jnp.broadcast_to(sums_ref[15:16, :], (8, 128)) * (1.0 / CHAN_TOTAL)
@@ -528,17 +537,21 @@
     before = jnp.where(inner, per_frame, jnp.where(step < per_frame, 0, 2 * per_frame))
     rows = pl.ds(pl.multiple_of((step - before) * size, size), size)
     mean, inv = coef_ref[0:1, :], coef_ref[1:2, :]
-    unit = (field_ref[...].astype(f32) - mean) * inv
-    taken = inv * (means[0:1, :] + unit * means[1:2, :])
-    for when, grad_ref in ((inner, inner_ref), (jnp.logical_not(inner), outer_ref)):
+    choices = (
+        (inner, inner_ref, inner_field_ref),
+        (jnp.logical_not(inner), outer_ref, outer_field_ref),
+    )
+    for when, grad_ref, field_ref in choices:
 
         @pl.when(when)
         def _():
+            unit = (field_ref[rows, :].astype(f32) - mean) * inv
+            taken = inv * (means[0:1, :] + unit * means[1:2, :])
             out_ref[...] = (grad_ref[rows, :] - taken).astype(bf16)
 
 
-def grad_of_field(inner, outer, field, coef, sums, block=288):
-    rows, width = field.shape
+def grad_of_field(inner, outer, inner_field, outer_field, coef, sums, block=288):
+    rows, width = 2 * inner.shape[0], inner.shape[1]
     tile = pl.BlockSpec((block, width), lambda i: (i, 0))
     return pl.pallas_call(
         result_kernel,
@@ -546,7 +559,8 @@
         in_specs=[
             IN_VMEM,
             IN_VMEM,
-            tile,
+            IN_VMEM,
+            IN_VMEM,
             pl.BlockSpec((8, width), lambda i: (0, 0)),
             pl.BlockSpec((16, 128), lambda i: (0, 0)),
         ],
@@ -555,7 +569,7 @@
         scratch_shapes=[pltpu.VMEM((8, width), f32)],
         compiler_params=params(12),
         cost_estimate=cost(rows * width * 9, rows * width * 10),
-    )(inner, outer, field, coef, sums)
+    )(inner, outer, inner_field, outer_field, coef, sums)
 
 
 def per_device(field, cotangent, gamma, beta, kernel):
@@ -584,7 +598,7 @@
     send_b, keep_b = taps_b(core, act_t, padded)
     got_b = swap(send_b, "core")
     none = jnp.zeros((8, width), f32)
-    inner, held, _ = gradient(keep_b, True, flat, padded, grad_inner, coef, none)
+    inner, inner_field, held, _ = gradient(keep_b, True, flat, padded, grad_inner, coef, none)
     kept, got = [keep_a, keep_b], [got_a, got_b]
     sums = [held]
     for step in range(3):
@@ -594,7 +608,7 @@
             lax.ppermute(merged[q][1], AXES, neighbours(NEAR[ORDERS[q][step]])) for q in range(2)
         ]
         if step == 0:
-            outer, _, sums = gradient(kept[0], False, flat, padded, kernel, coef, sums)
+            outer, outer_field, _, sums = gradient(kept[0], False, flat, padded, kernel, coef, sums)
             sums = [sums]
         elif step == 1:
             sums = [sums, swap(sums, "core"), swap(sums, "z0"), swap(sums, "core", "z0")]
@@ -605,7 +619,7 @@
     taps, sums = far_halve(taps, 2, "z1", own, off, sums)
     taps, sums = far_halve(taps, 1, "x1", own, off, sums)
     taps, sums = far_halve(taps, 0, "z2", own, off, sums)
-    field_grad = grad_of_field(inner, outer, flat, coef, sums)
+    field_grad = grad_of_field(inner, outer, inner_field, outer_field, coef, sums)
 
     got, sums = far_swap(taps, sums, "yh")
     taps = taps + got

time: 115 us -> 114 us (level)
  Pallas kernels: 48.2 us -> 47 us
where the time goes in v2:
time: 114 us
  Pallas kernels  47 us (41%)
  starting transfers between devices  44.7 us (39%)
  waiting for transfers between devices  19.1 us (17%)
    ppermute x12, starting transfers between devices, swap(): return lax.ppermute(value, AXES, chosen)  17.1 us
    ppermute x12, waiting for transfers between devices, swap(): return lax.ppermute(value, AXES, chosen)  16.2 us
    all_to_all x1, starting transfers between devices, per_device(): stats = lax.all_to_all(stats, ('tm', 'height'), 0, 0)  10.4 us
    pallas_call x2, Pallas kernels, gradient(): pl.pallas_call(functools.partial(gradient_kernel, inner), grid=(2,), in_s...  10.1 us
    pallas_call x1, Pallas kernels, taps_a(): pl.pallas_call(taps_a_kernel, in_specs=[IN_SMEM] + [IN_VMEM] * 2 + [ANYWH...  8.38 us
    pallas_call x1, Pallas kernels, inner_grad_act(): pl.pallas_call(grad_act_kernel, grid=(2,), in_specs=[part(0), part(1), pa...  8.02 us
    ppermute x6, starting transfers between devices, per_device(): lax.ppermute(merged[q][1], AXES, neighbours(NEAR[ORDERS[q][step]]))  7.46 us
    pallas_call x1, Pallas kernels, local_stats(): pl.pallas_call(stats_kernel, grid=(BLOCKS // 2,), in_specs=[IN_SMEM, pl.B...  6.37 us
  transfers between devices with their start and end apart: 21, of which 7 were waited for; matrix products, arithmetic and copies ran while one was open for 0% of the time, Pallas kernels for 23%

profile of v2, /device:TPU:2, one launch (start us, length us, event | category | flops | bytes accessed | tf_op | source)
XLA Modules:
  0.0 113.8 jit_solution(17553935918168646612)
XLA Ops:
  0.8 6.4 %shard_map.76 = (f32[64,2,128]{2,1,0:T(2,128)}, bf16[576,640]{1,0:T(8,128)(2,1)}, bf16[576,640]{1,0:T(8,128)(2,1)}) custom-call(s32[16]{0:T(128)S(1)} %stack.73.bits_ref, bf16[2304,640]{1,0:T(8,128)(2,1)} %bitcast.55, bf16[2304,640]{1,0:T(8,128)(2,1)} %bitcast.56, bf16[2304,640]{1,0:T(8,128)(2,1)} %bitcast.60, bf16[2304,640]{1,0:T(8,128)(2,1)} %bitcast.61), custom_call_target="tpu_custom_call" | custom-call | flops 5898240 | bytes 2949120 | tf_op jit(solution)/shard_map/pallas_call | solution.py:153
  7.2 3.8 %collective-permute-start = (bf16[576,640]{1,0:T(8,128)(2,1)}, bf16[576,640]{1,0:T(8,128)(2,1)}, u32[]{:S(2)}, u32[]{:S(2)}) collective-permute-start(bf16[576,640]{1,0:T(8,128)(2,1)} %get-tuple-element.35), channel_id=1, source_target_pairs={{0,2},{2,4},{4,6},{6,8},{8,10},{10,12},{12,14},{14,16},{16,18},{18... | collective-permute-start | bytes 2211848 | tf_op jit(solution)/shard_map/ppermute | solution.py:588
  11.0 5.8 %collective-permute-start.1 = (bf16[576,640]{1,0:T(8,128)(2,1)}, bf16[576,640]{1,0:T(8,128)(2,1)}, u32[]{:S(2)}, u32[]{:S(2)}) collective-permute-start(bf16[576,640]{1,0:T(8,128)(2,1)} %get-tuple-element.36), channel_id=1, source_target_pairs={{2,0},{4,2},{6,4},{8,6},{10,8},{12,10},{14,12},{16,14},{18,16},{20... | collective-permute-start | bytes 2211848 | tf_op jit(solution)/shard_map/ppermute | solution.py:589
  16.8 10.4 %all-to-all-start = ((f32[64,2,128]{2,1,0:T(2,128)}), f32[64,2,128]{2,1,0:T(2,128)S(1)}, u32[]{:S(2)}, u32[]{:S(2)}) async-start(f32[64,2,128]{2,1,0:T(2,128)} %get-tuple-element.34), calls=%async_computation | async-start | bytes 131072 | tf_op jit(solution)/shard_map/all_to_all | solution.py:590
  27.5 3.4 %shard_map.77.field_ref = bf16[640,2304]{1,0:T(8,128)(2,1)} custom-call(bf16[2304,640]{1,0:T(8,128)(2,1)S(1)} %bitcast.57), custom_call_target="tpu_custom_call" | custom-call | flops 1000000000 | bytes 10000000 | tf_op jit(solution)/shard_map/pallas_call | solution.py:188
  30.9 8.0 %shard_map.78.tie_ref.kernel_ref = f32[1152,640]{1,0:T(8,128)} custom-call(bf16[2304,640]{1,0:T(8,128)(2,1)} %bitcast.62, bf16[2304,640]{1,0:T(8,128)(2,1)} %bitcast.63, bf16[2304,640]{1,0:T(8,128)(2,1)} %bitcast.64, bf16[3,640,640]{2,1,0:T(8,128)(2,1)} %kernel_ref.3), custom_call_target="tpu_custom_call" | custom-call | flops 1000000000 | bytes 10000000 | tf_op jit(solution)/shard_map/pallas_call | solution.py:216
  38.9 8.4 %shard_map.79 = (f32[8,640]{1,0:T(8,128)S(1)}, bf16[640,2304]{1,0:T(8,128)(2,1)S(1)}, bf16[3456,640]{1,0:T(8,128)(2,1)S(1)}, bf16[32,80,128]{2,1,0:T(8,128)(2,1)S(1)}, f32[32,80,128]{2,1,0:T(8,128)S(1)}) custom-call(s32[1]{0:T(128)} %bitcast.core_ref, f32[64,2,128]{2,1,0:T(2,128)S(1)} %all-to-all-done.stats_ref, f32[8,640]{1,0:T(8,128)S(1)} %maximum_maximum_fusion.gain_ref, ...), custom_call_target="tpu_custom_call" | custom-call | flops 2831155200 | bytes 10000000 | tf_op jit(solution)/shard_map/pallas_call | solution.py:363
  47.3 4.1 %shard_map.80 = (bf16[32,80,128]{2,1,0:T(8,128)(2,1)S(1)}, f32[32,80,128]{2,1,0:T(8,128)S(1)}) custom-call(s32[1]{0:T(128)} %bitcast.core_ref, bf16[640,2304]{1,0:T(8,128)(2,1)S(1)} %get-tuple-element.37.act_ref, bf16[3456,640]{1,0:T(8,128)(2,1)S(1)} %get-tuple-element.38.padded_ref), custom_call_target="tpu_custom_call" | custom-call | flops 2831155200 | bytes 10000000 | tf_op jit(solution)/shard_map/pallas_call | solution.py:395
  52.0 3.4 %shard_map.81 = (f32[1152,640]{1,0:T(8,128)S(1)}, bf16[1152,640]{1,0:T(8,128)(2,1)S(1)}, f32[8,640]{1,0:T(8,128)S(1)}, f32[16,128]{1,0:T(8,128)}) custom-call(f32[32,80,128]{2,1,0:T(8,128)S(1)} %get-tuple-element.39.tie_ref.refs_2_, bf16[2304,640]{1,0:T(8,128)(2,1)S(1)} %bitcast.58, bf16[3456,640]{1,0:T(8,128)(2,1)S(1)} %get-tuple-element.38.padded_ref, ...), custom_call_target="tpu_custom_call" | custom-call | flops 1 | bytes 1 | tf_op jit(solution)/shard_map/pallas_call | solution.py:498
  56.3 3.1 %collective-permute-start.4 = (bf16[16,80,128]{2,1,0:T(8,128)(2,1)S(1)}, bf16[16,80,128]{2,1,0:T(8,128)(2,1)S(1)}, u32[]{:S(2)}, u32[]{:S(2)}) collective-permute-start(bf16[16,80,128]{2,1,0:T(8,128)(2,1)S(1)} %get-tuple-element.51), channel_id=1, source_target_pairs={{0,2},{1,3},{2,0},{3,1},{4,6},{5,7},{6,4},{7,5},{8,10},{9,11},{10,... | collective-permute-start | bytes 983048 | tf_op jit(solution)/shard_map/ppermute | solution.py:608
  59.9 6.7 %shard_map.83 = (f32[1152,640]{1,0:T(8,128)S(1)}, bf16[1152,640]{1,0:T(8,128)(2,1)S(1)}, f32[8,640]{1,0:T(8,128)}, f32[16,128]{1,0:T(8,128)S(1)}) custom-call(f32[16,80,128]{2,1,0:T(8,128)S(1)} %get-tuple-element.46.tie_ref.refs_0_, bf16[2304,640]{1,0:T(8,128)(2,1)S(1)} %bitcast.59, bf16[3456,640]{1,0:T(8,128)(2,1)S(1)} %get-tuple-element.38.padded_ref, ...), custom_call_target="tpu_custom_call" | custom-call | flops 1 | bytes 1 | tf_op jit(solution)/shard_map/pallas_call | solution.py:498
  67.3 1.5 %collective-permute-start.6 = (bf16[8,80,128]{2,1,0:T(8,128)(2,1)S(1)}, bf16[8,80,128]{2,1,0:T(8,128)(2,1)S(1)}, u32[]{:S(2)}, u32[]{:S(2)}) collective-permute-start(bf16[8,80,128]{2,1,0:T(8,128)(2,1)S(1)} %get-tuple-element.56), channel_id=1, source_target_pairs={{0,16},{1,17},{2,18},{3,19},{4,20},{5,21},{6,22},{7,23},{8,24},{9,... | collective-permute-start | bytes 491528 | tf_op jit(solution)/shard_map/ppermute | solution.py:608
  69.0 1.6 %collective-permute-start.10 = (f32[16,128]{1,0:T(8,128)S(1)}, f32[16,128]{1,0:T(8,128)S(1)}, u32[]{:S(2)}, u32[]{:S(2)}) collective-permute-start(f32[16,128]{1,0:T(8,128)S(1)} %get-tuple-element.59.refs_4_), channel_id=1, source_target_pairs={{0,66},{1,67},{2,64},{3,65},{4,70},{5,71},{6,68},{7,69},{8,74},{9,... | collective-permute-start | bytes 24584 | tf_op jit(solution)/shard_map/ppermute | solution.py:72
  72.4 2.3 %collective-permute-done.9.refs_6_ = f32[16,128]{1,0:T(8,128)S(1)} collective-permute-done((f32[16,128]{1,0:T(8,128)S(1)}, f32[16,128]{1,0:T(8,128)S(1)}, u32[]{:S(2)}, u32[]{:S(2)}) %collective-permute-start.9) | collective-permute-done | bytes 8224 | tf_op jit(solution)/shard_map/ppermute | solution.py:72
  75.2 1.7 %collective-permute-start.11 = (f32[16,128]{1,0:T(8,128)S(1)}, f32[16,128]{1,0:T(8,128)S(1)}, u32[]{:S(2)}, u32[]{:S(2)}) collective-permute-start(f32[16,128]{1,0:T(8,128)S(1)} %get-tuple-element.60), channel_id=1, source_target_pairs={{0,16},{1,17},{2,18},{3,19},{4,20},{5,21},{6,22},{7,23},{8,24},{9,... | collective-permute-start | bytes 24584 | tf_op jit(solution)/shard_map/ppermute | solution.py:72
  78.8 1.7 %collective-permute-start.15 = (bf16[4,80,128]{2,1,0:T(8,128)(2,1)S(1)}, bf16[4,80,128]{2,1,0:T(8,128)(2,1)S(1)}, u32[]{:S(2)}, u32[]{:S(2)}) collective-permute-start(bf16[4,80,128]{2,1,0:T(8,128)(2,1)S(1)} %get-tuple-element.64), channel_id=1, source_target_pairs={{0,16},{1,17},{2,18},{3,19},{4,20},{5,21},{6,22},{7,23},{8,24},{9,... | collective-permute-start | bytes 245768 | tf_op jit(solution)/shard_map/ppermute | solution.py:608
  83.3 1.6 %collective-permute-done.14 = bf16[4,80,128]{2,1,0:T(8,128)(2,1)S(1)} collective-permute-done((bf16[4,80,128]{2,1,0:T(8,128)(2,1)S(1)}, bf16[4,80,128]{2,1,0:T(8,128)(2,1)S(1)}, u32[]{:S(2)}, u32[]{:S(2)}) %collective-permute-start.14) | collective-permute-done | bytes 81952 | tf_op jit(solution)/shard_map/ppermute | solution.py:608
  85.0 3.8 %collective-permute-start.16 = (bf16[368,128]{1,0:T(8,128)(2,1)S(1)}, bf16[368,128]{1,0:T(8,128)(2,1)S(1)}, u32[]{:S(2)}, u32[]{:S(2)}) collective-permute-start(bf16[368,128]{1,0:T(8,128)(2,1)S(1)} %pad_maximum_fusion), channel_id=1, source_target_pairs={{0,4},{1,5},{2,6},{3,7},{4,0},{5,1},{6,2},{7,3},{8,12},{9,13},{10,... | collective-permute-start | bytes 282632 | tf_op jit(solution)/shard_map/ppermute | solution.py:72
  88.8 3.6 %collective-permute-done.16 = bf16[368,128]{1,0:T(8,128)(2,1)S(1)} collective-permute-done((bf16[368,128]{1,0:T(8,128)(2,1)S(1)}, bf16[368,128]{1,0:T(8,128)(2,1)S(1)}, u32[]{:S(2)}, u32[]{:S(2)}) %collective-permute-start.16) | collective-permute-done | bytes 94240 | tf_op jit(solution)/shard_map/ppermute | solution.py:72
  92.9 5.3 %collective-permute-done.17 = bf16[208,128]{1,0:T(8,128)(2,1)S(1)} collective-permute-done((bf16[208,128]{1,0:T(8,128)(2,1)S(1)}, bf16[208,128]{1,0:T(8,128)(2,1)S(1)}, u32[]{:S(2)}, u32[]{:S(2)}) %collective-permute-start.17) | collective-permute-done | bytes 53280 | tf_op jit(solution)/shard_map/ppermute | solution.py:72
  98.3 3.9 %collective-permute-start.18 = (bf16[128,128]{1,0:T(8,128)(2,1)S(1)}, bf16[128,128]{1,0:T(8,128)(2,1)S(1)}, u32[]{:S(2)}, u32[]{:S(2)}) collective-permute-start(bf16[128,128]{1,0:T(8,128)(2,1)S(1)} %pad_maximum_fusion.4), channel_id=1, source_target_pairs={{0,8},{1,9},{2,10},{3,11},{4,12},{5,13},{6,14},{7,15},{8,0},{9,1},... | collective-permute-start | bytes 98312 | tf_op jit(solution)/shard_map/ppermute | solution.py:72
  102.3 4.0 %collective-permute-done.18 = bf16[128,128]{1,0:T(8,128)(2,1)S(1)} collective-permute-done((bf16[128,128]{1,0:T(8,128)(2,1)S(1)}, bf16[128,128]{1,0:T(8,128)(2,1)S(1)}, u32[]{:S(2)}, u32[]{:S(2)}) %collective-permute-start.18) | collective-permute-done | bytes 32800 | tf_op jit(solution)/shard_map/ppermute | solution.py:72
  106.3 1.5 %collective-permute-start.19 = (bf16[128,128]{1,0:T(8,128)(2,1)S(1)}, bf16[128,128]{1,0:T(8,128)(2,1)S(1)}, u32[]{:S(2)}, u32[]{:S(2)}) collective-permute-start(bf16[128,128]{1,0:T(8,128)(2,1)S(1)} %pad_maximum_fusion.5), channel_id=1, source_target_pairs={{0,128},{1,129},{2,130},{3,131},{4,132},{5,133},{6,134},{7,135},{8... | collective-permute-start | bytes 98312 | tf_op jit(solution)/shard_map/ppermute | solution.py:72
  107.8 4.5 %shard_map.86 = bf16[2304,640]{1,0:T(8,128)(2,1)} custom-call(f32[1152,640]{1,0:T(8,128)S(1)} %get-tuple-element.41.inner_ref, f32[1152,640]{1,0:T(8,128)S(1)} %get-tuple-element.48.outer_ref, bf16[1152,640]{1,0:T(8,128)(2,1)S(1)} %get-tuple-element.49.inner_field_ref, bf16[1152,640]{1,0:T(8,128)(2,1)S(1)} %get-tuple-element.50.outer_field_ref, ...), custom_call_target="tpu_custom_call" | custom-call | flops 13271040 | bytes 14745600 | tf_op jit(solution)/shard_map/pallas_call | solution.py:556
  (84 shorter events, 12.2 us)
Async XLA Ops:
  0.7 26.5 %copy-start.3 = (f32[640]{0:T(1024)S(1)}, f32[640]{0:T(1024)}, u32[]{:S(2)}) copy-start(f32[640]{0:T(1024)} %param.7) | copy-start | bytes 7684
  0.8 26.5 %copy-start.4 = (f32[640]{0:T(1024)S(1)}, f32[640]{0:T(1024)}, u32[]{:S(2)}) copy-start(f32[640]{0:T(1024)} %param.8) | copy-start | bytes 7684
  0.8 26.7 %copy-start = (bf16[1,4,9,64,640]{4,3,2,1,0:T(8,128)(2,1)S(1)}, bf16[1,4,9,64,640]{4,3,2,1,0:T(8,128)(2,1)}, u32[]{:S(2)}) copy-start(bf16[1,4,9,64,640]{4,3,2,1,0:T(8,128)(2,1)} %param.5) | copy-start | bytes 8847364
  7.2 31.7 %collective-permute-start = (bf16[576,640]{1,0:T(8,128)(2,1)}, bf16[576,640]{1,0:T(8,128)(2,1)}, u32[]{:S(2)}, u32[]{:S(2)}) collective-permute-start(bf16[576,640]{1,0:T(8,128)(2,1)} %get-tuple-element.35), channel_id=1, source_target_pairs={{0,2},{2,4},{4,6},{6,8},{8,10},{10,12},{12,14},{14,16},{16,18},{18... | collective-permute-start | bytes 2211848 | tf_op jit(solution)/shard_map/ppermute | solution.py:588
  11.0 27.9 %collective-permute-start.1 = (bf16[576,640]{1,0:T(8,128)(2,1)}, bf16[576,640]{1,0:T(8,128)(2,1)}, u32[]{:S(2)}, u32[]{:S(2)}) collective-permute-start(bf16[576,640]{1,0:T(8,128)(2,1)} %get-tuple-element.36), channel_id=1, source_target_pairs={{2,0},{4,2},{6,4},{8,6},{10,8},{12,10},{14,12},{16,14},{18,16},{20... | collective-permute-start | bytes 2211848 | tf_op jit(solution)/shard_map/ppermute | solution.py:589
  16.8 22.1 %all-to-all-start = ((f32[64,2,128]{2,1,0:T(2,128)}), f32[64,2,128]{2,1,0:T(2,128)S(1)}, u32[]{:S(2)}, u32[]{:S(2)}) async-start(f32[64,2,128]{2,1,0:T(2,128)} %get-tuple-element.34), calls=%async_computation | async-start | bytes 131072 | tf_op jit(solution)/shard_map/all_to_all | solution.py:590
  51.4 4.0 %collective-permute-start.3 = (bf16[32,80,128]{2,1,0:T(8,128)(2,1)S(1)}, bf16[32,80,128]{2,1,0:T(8,128)(2,1)S(1)}, u32[]{:S(2)}, u32[]{:S(2)}) collective-permute-start(bf16[32,80,128]{2,1,0:T(8,128)(2,1)S(1)} %get-tuple-element.44), channel_id=1, source_target_pairs={{0,64},{1,65},{2,66},{3,67},{4,68},{5,69},{6,70},{7,71},{8,72},{9,... | collective-permute-start | bytes 1966088 | tf_op jit(solution)/shard_map/ppermute | solution.py:72
  51.5 3.9 %collective-permute-start.2 = (bf16[32,80,128]{2,1,0:T(8,128)(2,1)S(1)}, bf16[32,80,128]{2,1,0:T(8,128)(2,1)S(1)}, u32[]{:S(2)}, u32[]{:S(2)}) collective-permute-start(bf16[32,80,128]{2,1,0:T(8,128)(2,1)S(1)} %get-tuple-element.43), channel_id=1, source_target_pairs={{0,64},{1,65},{2,66},{3,67},{4,68},{5,69},{6,70},{7,71},{8,72},{9,... | collective-permute-start | bytes 1966088 | tf_op jit(solution)/shard_map/ppermute | solution.py:72
  56.3 10.4 %collective-permute-start.4 = (bf16[16,80,128]{2,1,0:T(8,128)(2,1)S(1)}, bf16[16,80,128]{2,1,0:T(8,128)(2,1)S(1)}, u32[]{:S(2)}, u32[]{:S(2)}) collective-permute-start(bf16[16,80,128]{2,1,0:T(8,128)(2,1)S(1)} %get-tuple-element.51), channel_id=1, source_target_pairs={{0,2},{1,3},{2,0},{3,1},{4,6},{5,7},{6,4},{7,5},{8,10},{9,11},{10,... | collective-permute-start | bytes 983048 | tf_op jit(solution)/shard_map/ppermute | solution.py:608
  59.3 7.3 %collective-permute-start.5 = (bf16[16,80,128]{2,1,0:T(8,128)(2,1)S(1)}, bf16[16,80,128]{2,1,0:T(8,128)(2,1)S(1)}, u32[]{:S(2)}, u32[]{:S(2)}) collective-permute-start(bf16[16,80,128]{2,1,0:T(8,128)(2,1)S(1)} %get-tuple-element.53), channel_id=1, source_target_pairs={{0,1},{1,0},{2,3},{3,2},{4,5},{5,4},{6,7},{7,6},{8,9},{9,8},{10,11... | collective-permute-start | bytes 983048 | tf_op jit(solution)/shard_map/ppermute | solution.py:608
  67.3 7.3 %collective-permute-start.6 = (bf16[8,80,128]{2,1,0:T(8,128)(2,1)S(1)}, bf16[8,80,128]{2,1,0:T(8,128)(2,1)S(1)}, u32[]{:S(2)}, u32[]{:S(2)}) collective-permute-start(bf16[8,80,128]{2,1,0:T(8,128)(2,1)S(1)} %get-tuple-element.56), channel_id=1, source_target_pairs={{0,16},{1,17},{2,18},{3,19},{4,20},{5,21},{6,22},{7,23},{8,24},{9,... | collective-permute-start | bytes 491528 | tf_op jit(solution)/shard_map/ppermute | solution.py:608
  68.8 5.8 %collective-permute-start.7 = (bf16[8,80,128]{2,1,0:T(8,128)(2,1)S(1)}, bf16[8,80,128]{2,1,0:T(8,128)(2,1)S(1)}, u32[]{:S(2)}, u32[]{:S(2)}) collective-permute-start(bf16[8,80,128]{2,1,0:T(8,128)(2,1)S(1)} %get-tuple-element.58), channel_id=1, source_target_pairs={{0,2},{1,3},{2,0},{3,1},{4,6},{5,7},{6,4},{7,5},{8,10},{9,11},{10,... | collective-permute-start | bytes 491528 | tf_op jit(solution)/shard_map/ppermute | solution.py:608
  69.0 3.3 %collective-permute-start.10 = (f32[16,128]{1,0:T(8,128)S(1)}, f32[16,128]{1,0:T(8,128)S(1)}, u32[]{:S(2)}, u32[]{:S(2)}) collective-permute-start(f32[16,128]{1,0:T(8,128)S(1)} %get-tuple-element.59.refs_4_), channel_id=1, source_target_pairs={{0,66},{1,67},{2,64},{3,65},{4,70},{5,71},{6,68},{7,69},{8,74},{9,... | collective-permute-start | bytes 24584 | tf_op jit(solution)/shard_map/ppermute | solution.py:72
  70.6 1.8 %collective-permute-start.8 = (f32[16,128]{1,0:T(8,128)S(1)}, f32[16,128]{1,0:T(8,128)S(1)}, u32[]{:S(2)}, u32[]{:S(2)}) collective-permute-start(f32[16,128]{1,0:T(8,128)S(1)} %get-tuple-element.59.refs_4_), channel_id=1, source_target_pairs={{0,64},{1,65},{2,66},{3,67},{4,68},{5,69},{6,70},{7,71},{8,72},{9,... | collective-permute-start | bytes 24584 | tf_op jit(solution)/shard_map/ppermute | solution.py:72
  71.0 3.7 %collective-permute-start.9 = (f32[16,128]{1,0:T(8,128)S(1)}, f32[16,128]{1,0:T(8,128)S(1)}, u32[]{:S(2)}, u32[]{:S(2)}) collective-permute-start(f32[16,128]{1,0:T(8,128)S(1)} %get-tuple-element.59.refs_4_), channel_id=1, source_target_pairs={{0,2},{1,3},{2,0},{3,1},{4,6},{5,7},{6,4},{7,5},{8,10},{9,11},{10,... | collective-permute-start | bytes 24584 | tf_op jit(solution)/shard_map/ppermute | solution.py:72
  75.2 5.7 %collective-permute-start.11 = (f32[16,128]{1,0:T(8,128)S(1)}, f32[16,128]{1,0:T(8,128)S(1)}, u32[]{:S(2)}, u32[]{:S(2)}) collective-permute-start(f32[16,128]{1,0:T(8,128)S(1)} %get-tuple-element.60), channel_id=1, source_target_pairs={{0,16},{1,17},{2,18},{3,19},{4,20},{5,21},{6,22},{7,23},{8,24},{9,... | collective-permute-start | bytes 24584 | tf_op jit(solution)/shard_map/ppermute | solution.py:72
  77.0 3.9 %collective-permute-start.12 = (f32[16,128]{1,0:T(8,128)S(1)}, f32[16,128]{1,0:T(8,128)S(1)}, u32[]{:S(2)}, u32[]{:S(2)}) collective-permute-start(f32[16,128]{1,0:T(8,128)S(1)} %get-tuple-element.60), channel_id=1, source_target_pairs={{0,1},{1,0},{2,3},{3,2},{4,5},{5,4},{6,7},{7,6},{8,9},{9,8},{10,11... | collective-permute-start | bytes 24584 | tf_op jit(solution)/shard_map/ppermute | solution.py:72
  77.4 4.5 %collective-permute-start.13 = (f32[16,128]{1,0:T(8,128)S(1)}, f32[16,128]{1,0:T(8,128)S(1)}, u32[]{:S(2)}, u32[]{:S(2)}) collective-permute-start(f32[16,128]{1,0:T(8,128)S(1)} %get-tuple-element.60), channel_id=1, source_target_pairs={{0,17},{1,16},{2,19},{3,18},{4,21},{5,20},{6,23},{7,22},{8,25},{9,... | collective-permute-start | bytes 24584 | tf_op jit(solution)/shard_map/ppermute | solution.py:72
  78.8 4.4 %collective-permute-start.15 = (bf16[4,80,128]{2,1,0:T(8,128)(2,1)S(1)}, bf16[4,80,128]{2,1,0:T(8,128)(2,1)S(1)}, u32[]{:S(2)}, u32[]{:S(2)}) collective-permute-start(bf16[4,80,128]{2,1,0:T(8,128)(2,1)S(1)} %get-tuple-element.64), channel_id=1, source_target_pairs={{0,16},{1,17},{2,18},{3,19},{4,20},{5,21},{6,22},{7,23},{8,24},{9,... | collective-permute-start | bytes 245768 | tf_op jit(solution)/shard_map/ppermute | solution.py:608
  80.5 4.4 %collective-permute-start.14 = (bf16[4,80,128]{2,1,0:T(8,128)(2,1)S(1)}, bf16[4,80,128]{2,1,0:T(8,128)(2,1)S(1)}, u32[]{:S(2)}, u32[]{:S(2)}) collective-permute-start(bf16[4,80,128]{2,1,0:T(8,128)(2,1)S(1)} %get-tuple-element.62), channel_id=1, source_target_pairs={{0,1},{1,0},{2,3},{3,2},{4,5},{5,4},{6,7},{7,6},{8,9},{9,8},{10,11... | collective-permute-start | bytes 245768 | tf_op jit(solution)/shard_map/ppermute | solution.py:608
  85.0 7.4 %collective-permute-start.16 = (bf16[368,128]{1,0:T(8,128)(2,1)S(1)}, bf16[368,128]{1,0:T(8,128)(2,1)S(1)}, u32[]{:S(2)}, u32[]{:S(2)}) collective-permute-start(bf16[368,128]{1,0:T(8,128)(2,1)S(1)} %pad_maximum_fusion), channel_id=1, source_target_pairs={{0,4},{1,5},{2,6},{3,7},{4,0},{5,1},{6,2},{7,3},{8,12},{9,13},{10,... | collective-permute-start | bytes 282632 | tf_op jit(solution)/shard_map/ppermute | solution.py:72
  92.5 5.7 %collective-permute-start.17 = (bf16[208,128]{1,0:T(8,128)(2,1)S(1)}, bf16[208,128]{1,0:T(8,128)(2,1)S(1)}, u32[]{:S(2)}, u32[]{:S(2)}) collective-permute-start(bf16[208,128]{1,0:T(8,128)(2,1)S(1)} %pad_maximum_fusion.1), channel_id=1, source_target_pairs={{0,32},{1,33},{2,34},{3,35},{4,36},{5,37},{6,38},{7,39},{8,40},{9,... | collective-permute-start | bytes 159752 | tf_op jit(solution)/shard_map/ppermute | solution.py:72
  98.3 7.9 %collective-permute-start.18 = (bf16[128,128]{1,0:T(8,128)(2,1)S(1)}, bf16[128,128]{1,0:T(8,128)(2,1)S(1)}, u32[]{:S(2)}, u32[]{:S(2)}) collective-permute-start(bf16[128,128]{1,0:T(8,128)(2,1)S(1)} %pad_maximum_fusion.4), channel_id=1, source_target_pairs={{0,8},{1,9},{2,10},{3,11},{4,12},{5,13},{6,14},{7,15},{8,0},{9,1},... | collective-permute-start | bytes 98312 | tf_op jit(solution)/shard_map/ppermute | solution.py:72
  106.3 6.0 %collective-permute-start.19 = (bf16[128,128]{1,0:T(8,128)(2,1)S(1)}, bf16[128,128]{1,0:T(8,128)(2,1)S(1)}, u32[]{:S(2)}, u32[]{:S(2)}) collective-permute-start(bf16[128,128]{1,0:T(8,128)(2,1)S(1)} %pad_maximum_fusion.5), channel_id=1, source_target_pairs={{0,128},{1,129},{2,130},{3,131},{4,132},{5,133},{6,134},{7,135},{8... | collective-permute-start | bytes 98312 | tf_op jit(solution)/shard_map/ppermute | solution.py:72
  (2 other events, 9.2 us)

commit v3 on v2

--- a/solution.py
+++ b/solution.py
@@ -312,7 +312,10 @@
         )
     pieces.append((after_ref, padded_ref.at[pl.ds(FRAME + rows, FRAME)]))
     copies = [pltpu.make_async_copy(*piece, sems.at[q]) for q, piece in enumerate(pieces)]
-    copies[0].start()
+    for q in [0, 1] + list(range(chunks, len(copies) - 2)) + list(range(2, chunks)):
+        copies[q].start()
+    for copy in copies[-2:]:
+        copy.start()
     total = jnp.sum(stats_ref[...], axis=0)
     mean = total[0:1] * (1.0 / 64)
     gaps = stats_ref[...] - mean[None]
@@ -329,10 +332,6 @@
         wide[q] = jnp.broadcast_to(coef[:, q : q + 1], (width, 128))
 
     copies[0].wait()
-    for q in [1] + list(range(chunks, len(copies) - 2)) + list(range(2, chunks)):
-        copies[q].start()
-    for copy in copies[-2:]:
-        copy.start()
 
     def activate(j):
         if j == 1:

time: 114 us -> 113 us (level)
  no operation moved by 1% of the time
where the time goes in v3:
time: 113 us
  Pallas kernels  46.1 us (41%)
  starting transfers between devices  44.7 us (40%)
  waiting for transfers between devices  19.1 us (17%)
    ppermute x12, starting transfers between devices, swap(): return lax.ppermute(value, AXES, chosen)  17.2 us
    ppermute x12, waiting for transfers between devices, swap(): return lax.ppermute(value, AXES, chosen)  16.2 us
    all_to_all x1, starting transfers between devices, per_device(): stats = lax.all_to_all(stats, ('tm', 'height'), 0, 0)  10.4 us
    pallas_call x2, Pallas kernels, gradient(): pl.pallas_call(functools.partial(gradient_kernel, inner), grid=(2,), in_s...  10.1 us
    pallas_call x1, Pallas kernels, inner_grad_act(): pl.pallas_call(grad_act_kernel, grid=(2,), in_specs=[part(0), part(1), pa...  8.02 us
    pallas_call x1, Pallas kernels, taps_a(): pl.pallas_call(taps_a_kernel, in_specs=[IN_SMEM] + [IN_VMEM] * 2 + [ANYWH...  7.48 us
    ppermute x6, starting transfers between devices, per_device(): lax.ppermute(merged[q][1], AXES, neighbours(NEAR[ORDERS[q][step]]))  7.46 us
    pallas_call x1, Pallas kernels, local_stats(): pl.pallas_call(stats_kernel, grid=(BLOCKS // 2,), in_specs=[IN_SMEM, pl.B...  6.37 us
  transfers between devices with their start and end apart: 21, of which 7 were waited for; matrix products, arithmetic and copies ran while one was open for 0% of the time, Pallas kernels for 23%

profile of v3, /device:TPU:2, one launch (start us, length us, event | category | flops | bytes accessed | tf_op | source)
XLA Modules:
  0.0 112.9 jit_solution(12874073452400440243)
XLA Ops:
  0.8 6.4 %shard_map.76 = (f32[64,2,128]{2,1,0:T(2,128)}, bf16[576,640]{1,0:T(8,128)(2,1)}, bf16[576,640]{1,0:T(8,128)(2,1)}) custom-call(s32[16]{0:T(128)S(1)} %stack.73.bits_ref, bf16[2304,640]{1,0:T(8,128)(2,1)} %bitcast.55, bf16[2304,640]{1,0:T(8,128)(2,1)} %bitcast.56, bf16[2304,640]{1,0:T(8,128)(2,1)} %bitcast.60, bf16[2304,640]{1,0:T(8,128)(2,1)} %bitcast.61), custom_call_target="tpu_custom_call" | custom-call | flops 5898240 | bytes 2949120 | tf_op jit(solution)/shard_map/pallas_call | solution.py:153
  7.2 3.8 %collective-permute-start = (bf16[576,640]{1,0:T(8,128)(2,1)}, bf16[576,640]{1,0:T(8,128)(2,1)}, u32[]{:S(2)}, u32[]{:S(2)}) collective-permute-start(bf16[576,640]{1,0:T(8,128)(2,1)} %get-tuple-element.35), channel_id=1, source_target_pairs={{0,2},{2,4},{4,6},{6,8},{8,10},{10,12},{12,14},{14,16},{16,18},{18... | collective-permute-start | bytes 2211848 | tf_op jit(solution)/shard_map/ppermute | solution.py:587
  11.0 5.8 %collective-permute-start.1 = (bf16[576,640]{1,0:T(8,128)(2,1)}, bf16[576,640]{1,0:T(8,128)(2,1)}, u32[]{:S(2)}, u32[]{:S(2)}) collective-permute-start(bf16[576,640]{1,0:T(8,128)(2,1)} %get-tuple-element.36), channel_id=1, source_target_pairs={{2,0},{4,2},{6,4},{8,6},{10,8},{12,10},{14,12},{16,14},{18,16},{20... | collective-permute-start | bytes 2211848 | tf_op jit(solution)/shard_map/ppermute | solution.py:588
  16.8 10.4 %all-to-all-start = ((f32[64,2,128]{2,1,0:T(2,128)}), f32[64,2,128]{2,1,0:T(2,128)S(1)}, u32[]{:S(2)}, u32[]{:S(2)}) async-start(f32[64,2,128]{2,1,0:T(2,128)} %get-tuple-element.34), calls=%async_computation | async-start | bytes 131072 | tf_op jit(solution)/shard_map/all_to_all | solution.py:589
  27.5 3.4 %shard_map.77.field_ref = bf16[640,2304]{1,0:T(8,128)(2,1)} custom-call(bf16[2304,640]{1,0:T(8,128)(2,1)S(1)} %bitcast.57), custom_call_target="tpu_custom_call" | custom-call | flops 1000000000 | bytes 10000000 | tf_op jit(solution)/shard_map/pallas_call | solution.py:188
  30.9 8.0 %shard_map.78.tie_ref.kernel_ref = f32[1152,640]{1,0:T(8,128)} custom-call(bf16[2304,640]{1,0:T(8,128)(2,1)} %bitcast.62, bf16[2304,640]{1,0:T(8,128)(2,1)} %bitcast.63, bf16[2304,640]{1,0:T(8,128)(2,1)} %bitcast.64, bf16[3,640,640]{2,1,0:T(8,128)(2,1)} %kernel_ref.3), custom_call_target="tpu_custom_call" | custom-call | flops 1000000000 | bytes 10000000 | tf_op jit(solution)/shard_map/pallas_call | solution.py:216
  38.9 7.5 %shard_map.79 = (f32[8,640]{1,0:T(8,128)S(1)}, bf16[640,2304]{1,0:T(8,128)(2,1)S(1)}, bf16[3456,640]{1,0:T(8,128)(2,1)S(1)}, bf16[32,80,128]{2,1,0:T(8,128)(2,1)S(1)}, f32[32,80,128]{2,1,0:T(8,128)S(1)}) custom-call(s32[1]{0:T(128)} %bitcast.core_ref, f32[64,2,128]{2,1,0:T(2,128)S(1)} %all-to-all-done.stats_ref, f32[8,640]{1,0:T(8,128)S(1)} %maximum_maximum_fusion.gain_ref, ...), custom_call_target="tpu_custom_call" | custom-call | flops 2831155200 | bytes 10000000 | tf_op jit(solution)/shard_map/pallas_call | solution.py:362
  46.4 4.1 %shard_map.80 = (bf16[32,80,128]{2,1,0:T(8,128)(2,1)S(1)}, f32[32,80,128]{2,1,0:T(8,128)S(1)}) custom-call(s32[1]{0:T(128)} %bitcast.core_ref, bf16[640,2304]{1,0:T(8,128)(2,1)S(1)} %get-tuple-element.37.act_ref, bf16[3456,640]{1,0:T(8,128)(2,1)S(1)} %get-tuple-element.38.padded_ref), custom_call_target="tpu_custom_call" | custom-call | flops 2831155200 | bytes 10000000 | tf_op jit(solution)/shard_map/pallas_call | solution.py:394
  51.1 3.4 %shard_map.81 = (f32[1152,640]{1,0:T(8,128)S(1)}, bf16[1152,640]{1,0:T(8,128)(2,1)S(1)}, f32[8,640]{1,0:T(8,128)S(1)}, f32[16,128]{1,0:T(8,128)}) custom-call(f32[32,80,128]{2,1,0:T(8,128)S(1)} %get-tuple-element.39.tie_ref.refs_2_, bf16[2304,640]{1,0:T(8,128)(2,1)S(1)} %bitcast.58, bf16[3456,640]{1,0:T(8,128)(2,1)S(1)} %get-tuple-element.38.padded_ref, ...), custom_call_target="tpu_custom_call" | custom-call | flops 1 | bytes 1 | tf_op jit(solution)/shard_map/pallas_call | solution.py:497
  55.4 3.1 %collective-permute-start.4 = (bf16[16,80,128]{2,1,0:T(8,128)(2,1)S(1)}, bf16[16,80,128]{2,1,0:T(8,128)(2,1)S(1)}, u32[]{:S(2)}, u32[]{:S(2)}) collective-permute-start(bf16[16,80,128]{2,1,0:T(8,128)(2,1)S(1)} %get-tuple-element.51), channel_id=1, source_target_pairs={{0,2},{1,3},{2,0},{3,1},{4,6},{5,7},{6,4},{7,5},{8,10},{9,11},{10,... | collective-permute-start | bytes 983048 | tf_op jit(solution)/shard_map/ppermute | solution.py:607
  59.0 6.7 %shard_map.83 = (f32[1152,640]{1,0:T(8,128)S(1)}, bf16[1152,640]{1,0:T(8,128)(2,1)S(1)}, f32[8,640]{1,0:T(8,128)}, f32[16,128]{1,0:T(8,128)S(1)}) custom-call(f32[16,80,128]{2,1,0:T(8,128)S(1)} %get-tuple-element.46.tie_ref.refs_0_, bf16[2304,640]{1,0:T(8,128)(2,1)S(1)} %bitcast.59, bf16[3456,640]{1,0:T(8,128)(2,1)S(1)} %get-tuple-element.38.padded_ref, ...), custom_call_target="tpu_custom_call" | custom-call | flops 1 | bytes 1 | tf_op jit(solution)/shard_map/pallas_call | solution.py:497
  66.4 1.5 %collective-permute-start.6 = (bf16[8,80,128]{2,1,0:T(8,128)(2,1)S(1)}, bf16[8,80,128]{2,1,0:T(8,128)(2,1)S(1)}, u32[]{:S(2)}, u32[]{:S(2)}) collective-permute-start(bf16[8,80,128]{2,1,0:T(8,128)(2,1)S(1)} %get-tuple-element.56), channel_id=1, source_target_pairs={{0,16},{1,17},{2,18},{3,19},{4,20},{5,21},{6,22},{7,23},{8,24},{9,... | collective-permute-start | bytes 491528 | tf_op jit(solution)/shard_map/ppermute | solution.py:607
  68.1 1.6 %collective-permute-start.10 = (f32[16,128]{1,0:T(8,128)S(1)}, f32[16,128]{1,0:T(8,128)S(1)}, u32[]{:S(2)}, u32[]{:S(2)}) collective-permute-start(f32[16,128]{1,0:T(8,128)S(1)} %get-tuple-element.59.refs_4_), channel_id=1, source_target_pairs={{0,66},{1,67},{2,64},{3,65},{4,70},{5,71},{6,68},{7,69},{8,74},{9,... | collective-permute-start | bytes 24584 | tf_op jit(solution)/shard_map/ppermute | solution.py:72
  71.5 2.2 %collective-permute-done.9.refs_6_ = f32[16,128]{1,0:T(8,128)S(1)} collective-permute-done((f32[16,128]{1,0:T(8,128)S(1)}, f32[16,128]{1,0:T(8,128)S(1)}, u32[]{:S(2)}, u32[]{:S(2)}) %collective-permute-start.9) | collective-permute-done | bytes 8224 | tf_op jit(solution)/shard_map/ppermute | solution.py:72
  74.3 1.8 %collective-permute-start.11 = (f32[16,128]{1,0:T(8,128)S(1)}, f32[16,128]{1,0:T(8,128)S(1)}, u32[]{:S(2)}, u32[]{:S(2)}) collective-permute-start(f32[16,128]{1,0:T(8,128)S(1)} %get-tuple-element.60), channel_id=1, source_target_pairs={{0,16},{1,17},{2,18},{3,19},{4,20},{5,21},{6,22},{7,23},{8,24},{9,... | collective-permute-start | bytes 24584 | tf_op jit(solution)/shard_map/ppermute | solution.py:72
  77.9 1.7 %collective-permute-start.15 = (bf16[4,80,128]{2,1,0:T(8,128)(2,1)S(1)}, bf16[4,80,128]{2,1,0:T(8,128)(2,1)S(1)}, u32[]{:S(2)}, u32[]{:S(2)}) collective-permute-start(bf16[4,80,128]{2,1,0:T(8,128)(2,1)S(1)} %get-tuple-element.64), channel_id=1, source_target_pairs={{0,16},{1,17},{2,18},{3,19},{4,20},{5,21},{6,22},{7,23},{8,24},{9,... | collective-permute-start | bytes 245768 | tf_op jit(solution)/shard_map/ppermute | solution.py:607
  82.4 1.6 %collective-permute-done.14 = bf16[4,80,128]{2,1,0:T(8,128)(2,1)S(1)} collective-permute-done((bf16[4,80,128]{2,1,0:T(8,128)(2,1)S(1)}, bf16[4,80,128]{2,1,0:T(8,128)(2,1)S(1)}, u32[]{:S(2)}, u32[]{:S(2)}) %collective-permute-start.14) | collective-permute-done | bytes 81952 | tf_op jit(solution)/shard_map/ppermute | solution.py:607
  84.1 3.8 %collective-permute-start.16 = (bf16[368,128]{1,0:T(8,128)(2,1)S(1)}, bf16[368,128]{1,0:T(8,128)(2,1)S(1)}, u32[]{:S(2)}, u32[]{:S(2)}) collective-permute-start(bf16[368,128]{1,0:T(8,128)(2,1)S(1)} %pad_maximum_fusion), channel_id=1, source_target_pairs={{0,4},{1,5},{2,6},{3,7},{4,0},{5,1},{6,2},{7,3},{8,12},{9,13},{10,... | collective-permute-start | bytes 282632 | tf_op jit(solution)/shard_map/ppermute | solution.py:72
  87.9 3.6 %collective-permute-done.16 = bf16[368,128]{1,0:T(8,128)(2,1)S(1)} collective-permute-done((bf16[368,128]{1,0:T(8,128)(2,1)S(1)}, bf16[368,128]{1,0:T(8,128)(2,1)S(1)}, u32[]{:S(2)}, u32[]{:S(2)}) %collective-permute-start.16) | collective-permute-done | bytes 94240 | tf_op jit(solution)/shard_map/ppermute | solution.py:72
  92.0 5.3 %collective-permute-done.17 = bf16[208,128]{1,0:T(8,128)(2,1)S(1)} collective-permute-done((bf16[208,128]{1,0:T(8,128)(2,1)S(1)}, bf16[208,128]{1,0:T(8,128)(2,1)S(1)}, u32[]{:S(2)}, u32[]{:S(2)}) %collective-permute-start.17) | collective-permute-done | bytes 53280 | tf_op jit(solution)/shard_map/ppermute | solution.py:72
  97.4 4.0 %collective-permute-start.18 = (bf16[128,128]{1,0:T(8,128)(2,1)S(1)}, bf16[128,128]{1,0:T(8,128)(2,1)S(1)}, u32[]{:S(2)}, u32[]{:S(2)}) collective-permute-start(bf16[128,128]{1,0:T(8,128)(2,1)S(1)} %pad_maximum_fusion.4), channel_id=1, source_target_pairs={{0,8},{1,9},{2,10},{3,11},{4,12},{5,13},{6,14},{7,15},{8,0},{9,1},... | collective-permute-start | bytes 98312 | tf_op jit(solution)/shard_map/ppermute | solution.py:72
  101.4 3.9 %collective-permute-done.18 = bf16[128,128]{1,0:T(8,128)(2,1)S(1)} collective-permute-done((bf16[128,128]{1,0:T(8,128)(2,1)S(1)}, bf16[128,128]{1,0:T(8,128)(2,1)S(1)}, u32[]{:S(2)}, u32[]{:S(2)}) %collective-permute-start.18) | collective-permute-done | bytes 32800 | tf_op jit(solution)/shard_map/ppermute | solution.py:72
  105.4 1.5 %collective-permute-start.19 = (bf16[128,128]{1,0:T(8,128)(2,1)S(1)}, bf16[128,128]{1,0:T(8,128)(2,1)S(1)}, u32[]{:S(2)}, u32[]{:S(2)}) collective-permute-start(bf16[128,128]{1,0:T(8,128)(2,1)S(1)} %pad_maximum_fusion.5), channel_id=1, source_target_pairs={{0,128},{1,129},{2,130},{3,131},{4,132},{5,133},{6,134},{7,135},{8... | collective-permute-start | bytes 98312 | tf_op jit(solution)/shard_map/ppermute | solution.py:72
  106.9 4.5 %shard_map.86 = bf16[2304,640]{1,0:T(8,128)(2,1)} custom-call(f32[1152,640]{1,0:T(8,128)S(1)} %get-tuple-element.41.inner_ref, f32[1152,640]{1,0:T(8,128)S(1)} %get-tuple-element.48.outer_ref, bf16[1152,640]{1,0:T(8,128)(2,1)S(1)} %get-tuple-element.49.inner_field_ref, bf16[1152,640]{1,0:T(8,128)(2,1)S(1)} %get-tuple-element.50.outer_field_ref, ...), custom_call_target="tpu_custom_call" | custom-call | flops 13271040 | bytes 14745600 | tf_op jit(solution)/shard_map/pallas_call | solution.py:555
  (84 shorter events, 12.2 us)
Async XLA Ops:
  0.7 26.5 %copy-start.3 = (f32[640]{0:T(1024)S(1)}, f32[640]{0:T(1024)}, u32[]{:S(2)}) copy-start(f32[640]{0:T(1024)} %param.7) | copy-start | bytes 7684
  0.8 26.5 %copy-start.4 = (f32[640]{0:T(1024)S(1)}, f32[640]{0:T(1024)}, u32[]{:S(2)}) copy-start(f32[640]{0:T(1024)} %param.8) | copy-start | bytes 7684
  0.8 26.7 %copy-start = (bf16[1,4,9,64,640]{4,3,2,1,0:T(8,128)(2,1)S(1)}, bf16[1,4,9,64,640]{4,3,2,1,0:T(8,128)(2,1)}, u32[]{:S(2)}) copy-start(bf16[1,4,9,64,640]{4,3,2,1,0:T(8,128)(2,1)} %param.5) | copy-start | bytes 8847364
  7.2 31.7 %collective-permute-start = (bf16[576,640]{1,0:T(8,128)(2,1)}, bf16[576,640]{1,0:T(8,128)(2,1)}, u32[]{:S(2)}, u32[]{:S(2)}) collective-permute-start(bf16[576,640]{1,0:T(8,128)(2,1)} %get-tuple-element.35), channel_id=1, source_target_pairs={{0,2},{2,4},{4,6},{6,8},{8,10},{10,12},{12,14},{14,16},{16,18},{18... | collective-permute-start | bytes 2211848 | tf_op jit(solution)/shard_map/ppermute | solution.py:587
  11.0 27.9 %collective-permute-start.1 = (bf16[576,640]{1,0:T(8,128)(2,1)}, bf16[576,640]{1,0:T(8,128)(2,1)}, u32[]{:S(2)}, u32[]{:S(2)}) collective-permute-start(bf16[576,640]{1,0:T(8,128)(2,1)} %get-tuple-element.36), channel_id=1, source_target_pairs={{2,0},{4,2},{6,4},{8,6},{10,8},{12,10},{14,12},{16,14},{18,16},{20... | collective-permute-start | bytes 2211848 | tf_op jit(solution)/shard_map/ppermute | solution.py:588
  16.8 22.1 %all-to-all-start = ((f32[64,2,128]{2,1,0:T(2,128)}), f32[64,2,128]{2,1,0:T(2,128)S(1)}, u32[]{:S(2)}, u32[]{:S(2)}) async-start(f32[64,2,128]{2,1,0:T(2,128)} %get-tuple-element.34), calls=%async_computation | async-start | bytes 131072 | tf_op jit(solution)/shard_map/all_to_all | solution.py:589
  50.5 4.0 %collective-permute-start.3 = (bf16[32,80,128]{2,1,0:T(8,128)(2,1)S(1)}, bf16[32,80,128]{2,1,0:T(8,128)(2,1)S(1)}, u32[]{:S(2)}, u32[]{:S(2)}) collective-permute-start(bf16[32,80,128]{2,1,0:T(8,128)(2,1)S(1)} %get-tuple-element.44), channel_id=1, source_target_pairs={{0,64},{1,65},{2,66},{3,67},{4,68},{5,69},{6,70},{7,71},{8,72},{9,... | collective-permute-start | bytes 1966088 | tf_op jit(solution)/shard_map/ppermute | solution.py:72
  50.6 3.9 %collective-permute-start.2 = (bf16[32,80,128]{2,1,0:T(8,128)(2,1)S(1)}, bf16[32,80,128]{2,1,0:T(8,128)(2,1)S(1)}, u32[]{:S(2)}, u32[]{:S(2)}) collective-permute-start(bf16[32,80,128]{2,1,0:T(8,128)(2,1)S(1)} %get-tuple-element.43), channel_id=1, source_target_pairs={{0,64},{1,65},{2,66},{3,67},{4,68},{5,69},{6,70},{7,71},{8,72},{9,... | collective-permute-start | bytes 1966088 | tf_op jit(solution)/shard_map/ppermute | solution.py:72
  55.4 10.4 %collective-permute-start.4 = (bf16[16,80,128]{2,1,0:T(8,128)(2,1)S(1)}, bf16[16,80,128]{2,1,0:T(8,128)(2,1)S(1)}, u32[]{:S(2)}, u32[]{:S(2)}) collective-permute-start(bf16[16,80,128]{2,1,0:T(8,128)(2,1)S(1)} %get-tuple-element.51), channel_id=1, source_target_pairs={{0,2},{1,3},{2,0},{3,1},{4,6},{5,7},{6,4},{7,5},{8,10},{9,11},{10,... | collective-permute-start | bytes 983048 | tf_op jit(solution)/shard_map/ppermute | solution.py:607
  58.4 7.3 %collective-permute-start.5 = (bf16[16,80,128]{2,1,0:T(8,128)(2,1)S(1)}, bf16[16,80,128]{2,1,0:T(8,128)(2,1)S(1)}, u32[]{:S(2)}, u32[]{:S(2)}) collective-permute-start(bf16[16,80,128]{2,1,0:T(8,128)(2,1)S(1)} %get-tuple-element.53), channel_id=1, source_target_pairs={{0,1},{1,0},{2,3},{3,2},{4,5},{5,4},{6,7},{7,6},{8,9},{9,8},{10,11... | collective-permute-start | bytes 983048 | tf_op jit(solution)/shard_map/ppermute | solution.py:607
  66.4 7.3 %collective-permute-start.6 = (bf16[8,80,128]{2,1,0:T(8,128)(2,1)S(1)}, bf16[8,80,128]{2,1,0:T(8,128)(2,1)S(1)}, u32[]{:S(2)}, u32[]{:S(2)}) collective-permute-start(bf16[8,80,128]{2,1,0:T(8,128)(2,1)S(1)} %get-tuple-element.56), channel_id=1, source_target_pairs={{0,16},{1,17},{2,18},{3,19},{4,20},{5,21},{6,22},{7,23},{8,24},{9,... | collective-permute-start | bytes 491528 | tf_op jit(solution)/shard_map/ppermute | solution.py:607
  67.9 5.8 %collective-permute-start.7 = (bf16[8,80,128]{2,1,0:T(8,128)(2,1)S(1)}, bf16[8,80,128]{2,1,0:T(8,128)(2,1)S(1)}, u32[]{:S(2)}, u32[]{:S(2)}) collective-permute-start(bf16[8,80,128]{2,1,0:T(8,128)(2,1)S(1)} %get-tuple-element.58), channel_id=1, source_target_pairs={{0,2},{1,3},{2,0},{3,1},{4,6},{5,7},{6,4},{7,5},{8,10},{9,11},{10,... | collective-permute-start | bytes 491528 | tf_op jit(solution)/shard_map/ppermute | solution.py:607
  68.1 3.3 %collective-permute-start.10 = (f32[16,128]{1,0:T(8,128)S(1)}, f32[16,128]{1,0:T(8,128)S(1)}, u32[]{:S(2)}, u32[]{:S(2)}) collective-permute-start(f32[16,128]{1,0:T(8,128)S(1)} %get-tuple-element.59.refs_4_), channel_id=1, source_target_pairs={{0,66},{1,67},{2,64},{3,65},{4,70},{5,71},{6,68},{7,69},{8,74},{9,... | collective-permute-start | bytes 24584 | tf_op jit(solution)/shard_map/ppermute | solution.py:72
  69.7 1.8 %collective-permute-start.8 = (f32[16,128]{1,0:T(8,128)S(1)}, f32[16,128]{1,0:T(8,128)S(1)}, u32[]{:S(2)}, u32[]{:S(2)}) collective-permute-start(f32[16,128]{1,0:T(8,128)S(1)} %get-tuple-element.59.refs_4_), channel_id=1, source_target_pairs={{0,64},{1,65},{2,66},{3,67},{4,68},{5,69},{6,70},{7,71},{8,72},{9,... | collective-permute-start | bytes 24584 | tf_op jit(solution)/shard_map/ppermute | solution.py:72
  70.1 3.7 %collective-permute-start.9 = (f32[16,128]{1,0:T(8,128)S(1)}, f32[16,128]{1,0:T(8,128)S(1)}, u32[]{:S(2)}, u32[]{:S(2)}) collective-permute-start(f32[16,128]{1,0:T(8,128)S(1)} %get-tuple-element.59.refs_4_), channel_id=1, source_target_pairs={{0,2},{1,3},{2,0},{3,1},{4,6},{5,7},{6,4},{7,5},{8,10},{9,11},{10,... | collective-permute-start | bytes 24584 | tf_op jit(solution)/shard_map/ppermute | solution.py:72
  74.3 5.7 %collective-permute-start.11 = (f32[16,128]{1,0:T(8,128)S(1)}, f32[16,128]{1,0:T(8,128)S(1)}, u32[]{:S(2)}, u32[]{:S(2)}) collective-permute-start(f32[16,128]{1,0:T(8,128)S(1)} %get-tuple-element.60), channel_id=1, source_target_pairs={{0,16},{1,17},{2,18},{3,19},{4,20},{5,21},{6,22},{7,23},{8,24},{9,... | collective-permute-start | bytes 24584 | tf_op jit(solution)/shard_map/ppermute | solution.py:72
  76.1 3.9 %collective-permute-start.12 = (f32[16,128]{1,0:T(8,128)S(1)}, f32[16,128]{1,0:T(8,128)S(1)}, u32[]{:S(2)}, u32[]{:S(2)}) collective-permute-start(f32[16,128]{1,0:T(8,128)S(1)} %get-tuple-element.60), channel_id=1, source_target_pairs={{0,1},{1,0},{2,3},{3,2},{4,5},{5,4},{6,7},{7,6},{8,9},{9,8},{10,11... | collective-permute-start | bytes 24584 | tf_op jit(solution)/shard_map/ppermute | solution.py:72
  76.5 4.5 %collective-permute-start.13 = (f32[16,128]{1,0:T(8,128)S(1)}, f32[16,128]{1,0:T(8,128)S(1)}, u32[]{:S(2)}, u32[]{:S(2)}) collective-permute-start(f32[16,128]{1,0:T(8,128)S(1)} %get-tuple-element.60), channel_id=1, source_target_pairs={{0,17},{1,16},{2,19},{3,18},{4,21},{5,20},{6,23},{7,22},{8,25},{9,... | collective-permute-start | bytes 24584 | tf_op jit(solution)/shard_map/ppermute | solution.py:72
  77.9 4.4 %collective-permute-start.15 = (bf16[4,80,128]{2,1,0:T(8,128)(2,1)S(1)}, bf16[4,80,128]{2,1,0:T(8,128)(2,1)S(1)}, u32[]{:S(2)}, u32[]{:S(2)}) collective-permute-start(bf16[4,80,128]{2,1,0:T(8,128)(2,1)S(1)} %get-tuple-element.64), channel_id=1, source_target_pairs={{0,16},{1,17},{2,18},{3,19},{4,20},{5,21},{6,22},{7,23},{8,24},{9,... | collective-permute-start | bytes 245768 | tf_op jit(solution)/shard_map/ppermute | solution.py:607
  79.6 4.4 %collective-permute-start.14 = (bf16[4,80,128]{2,1,0:T(8,128)(2,1)S(1)}, bf16[4,80,128]{2,1,0:T(8,128)(2,1)S(1)}, u32[]{:S(2)}, u32[]{:S(2)}) collective-permute-start(bf16[4,80,128]{2,1,0:T(8,128)(2,1)S(1)} %get-tuple-element.62), channel_id=1, source_target_pairs={{0,1},{1,0},{2,3},{3,2},{4,5},{5,4},{6,7},{7,6},{8,9},{9,8},{10,11... | collective-permute-start | bytes 245768 | tf_op jit(solution)/shard_map/ppermute | solution.py:607
  84.1 7.4 %collective-permute-start.16 = (bf16[368,128]{1,0:T(8,128)(2,1)S(1)}, bf16[368,128]{1,0:T(8,128)(2,1)S(1)}, u32[]{:S(2)}, u32[]{:S(2)}) collective-permute-start(bf16[368,128]{1,0:T(8,128)(2,1)S(1)} %pad_maximum_fusion), channel_id=1, source_target_pairs={{0,4},{1,5},{2,6},{3,7},{4,0},{5,1},{6,2},{7,3},{8,12},{9,13},{10,... | collective-permute-start | bytes 282632 | tf_op jit(solution)/shard_map/ppermute | solution.py:72
  91.6 5.7 %collective-permute-start.17 = (bf16[208,128]{1,0:T(8,128)(2,1)S(1)}, bf16[208,128]{1,0:T(8,128)(2,1)S(1)}, u32[]{:S(2)}, u32[]{:S(2)}) collective-permute-start(bf16[208,128]{1,0:T(8,128)(2,1)S(1)} %pad_maximum_fusion.1), channel_id=1, source_target_pairs={{0,32},{1,33},{2,34},{3,35},{4,36},{5,37},{6,38},{7,39},{8,40},{9,... | collective-permute-start | bytes 159752 | tf_op jit(solution)/shard_map/ppermute | solution.py:72
  97.4 7.9 %collective-permute-start.18 = (bf16[128,128]{1,0:T(8,128)(2,1)S(1)}, bf16[128,128]{1,0:T(8,128)(2,1)S(1)}, u32[]{:S(2)}, u32[]{:S(2)}) collective-permute-start(bf16[128,128]{1,0:T(8,128)(2,1)S(1)} %pad_maximum_fusion.4), channel_id=1, source_target_pairs={{0,8},{1,9},{2,10},{3,11},{4,12},{5,13},{6,14},{7,15},{8,0},{9,1},... | collective-permute-start | bytes 98312 | tf_op jit(solution)/shard_map/ppermute | solution.py:72
  105.4 6.0 %collective-permute-start.19 = (bf16[128,128]{1,0:T(8,128)(2,1)S(1)}, bf16[128,128]{1,0:T(8,128)(2,1)S(1)}, u32[]{:S(2)}, u32[]{:S(2)}) collective-permute-start(bf16[128,128]{1,0:T(8,128)(2,1)S(1)} %pad_maximum_fusion.5), channel_id=1, source_target_pairs={{0,128},{1,129},{2,130},{3,131},{4,132},{5,133},{6,134},{7,135},{8... | collective-permute-start | bytes 98312 | tf_op jit(solution)/shard_map/ppermute | solution.py:72
  (2 other events, 9.2 us)
